TPU v7x, 512 devices: a whole 4x4x16 slice. The times are simulated.
512 devices in a mesh: stn: 32 (over z, x_hi), day: 16 (over x_lo, y, core).
Axes of the slice: x: 4 (x_hi: 2, x_lo: 2; x = x_hi * 2 + x_lo), y: 4, z: 16, core: 2. Of those that a mesh axis runs over, the one named last changes fastest.
Arguments:
- records: bfloat16 [1024, 128, 6000], P('stn', 'day'), may hold values from -6 to 6
- offsets: int32 [16], replicated, may hold values from 0 to 15, each once
- pair_order: int32 [1024], replicated, may hold values from 0 to 1023, each once
Outputs:
- stacks: float32 [16, 101, 32768], P(None, None, ('stn', 'day'))
Inputs may be any that keep to these rules, and one draw needn't show every extreme that they name: offsets is a permutation of 0 to 15. pair_order is a permutation of 0 to 1023.
All inputs are finite; a program needn't handle non-finite values.
Results may differ from a plain program's by a relative error of at most 0.022.
Values may be sent and summed in bfloat16 or wider, within the bound.
No kernel may reach another device: no remote copies, remote signals or barrier semaphores. Data moves between devices by JAX's collectives and lax.ppermute only.
A program may use at most 64 MiB of HBM per device.

v0:
```python
import math

import jax
import jax.numpy as jnp
from jax import lax
from jax.sharding import PartitionSpec as P

NT = 6000
NB = 128
K0 = 30
LAGS = 101


def from_behind(value, axis, steps):
    count = lax.axis_size(axis)
    pairs = [(source, (source + steps) % count) for source in range(count)]
    return lax.ppermute(value, axis, pairs)


def phase_rows(column_values):
    band_bins = jnp.arange(NB, dtype=jnp.int32) + K0
    phase_turns = band_bins[:, None] * column_values[None, :] % NT
    phase_angle = 2.0 * math.pi / NT * phase_turns.astype(jnp.float32)
    return jnp.concatenate([jnp.cos(phase_angle), -jnp.sin(phase_angle)], axis=0).astype(
        jnp.bfloat16
    )


def spectra_of(block, band_rows):
    station_count = block.shape[0]
    day_count = block.shape[1]
    series = block.astype(jnp.float32).reshape(station_count * day_count, NT)
    series = series - jnp.mean(series, axis=1, keepdims=True)
    series = series / jnp.sqrt(jnp.mean(series * series, axis=1, keepdims=True) + 1e-06)
    series = series.astype(jnp.bfloat16)
    raw = lax.dot_general(
        series, band_rows, (((1,), (1,)), ((), ())), preferred_element_type=jnp.float32
    )
    raw = raw / jnp.sqrt(jnp.sum(raw * raw, axis=1, keepdims=True) / NB + 1e-06)
    spectra = raw.astype(jnp.bfloat16).reshape(station_count, day_count, 2, NB)
    return jnp.transpose(spectra, (0, 2, 1, 3)).reshape(station_count, 2 * day_count, NB)


def correlate(own_spectra, partner, lag_rows, weight_scale):
    half_count = own_spectra.shape[1] // 2
    station_count = own_spectra.shape[0]
    turned = jnp.concatenate([own_spectra[:, half_count:], -own_spectra[:, :half_count]], axis=1)
    real_part = jnp.einsum("ick,jck->ijk", own_spectra, partner, preferred_element_type=jnp.float32)
    imag_part = jnp.einsum("ick,jck->ijk", turned, partner, preferred_element_type=jnp.float32)
    cross_spec = jnp.stack([real_part, imag_part], axis=2).reshape(
        station_count * station_count, 2 * NB
    )
    cross_spec = cross_spec.astype(jnp.bfloat16)
    lagged = lax.dot_general(
        lag_rows, cross_spec, (((0,), (1,)), ((), ())), preferred_element_type=jnp.float32
    )
    return weight_scale * lagged


def shards(records, offsets, pair_order):
    day_count = lax.axis_size("day")
    own_spectra = spectra_of(records, phase_rows(jnp.arange(NT, dtype=jnp.int32)))
    lag_rows = phase_rows(jnp.arange(LAGS, dtype=jnp.int32) - LAGS // 2)
    weight_scale = 1.0 / math.sqrt(NB * records.shape[1] * day_count)
    round_count = offsets.shape[0]
    pair_count = own_spectra.shape[0] * own_spectra.shape[0]
    share_width = pair_count // day_count
    round_numbers = jnp.arange(round_count, dtype=jnp.int32)

    def round_body(round_step, carry):
        current, result = carry
        current = from_behind(current, "stn", 1)
        slot_index = jnp.sum(jnp.where(offsets == round_step, round_numbers, 0))
        day_partial = correlate(own_spectra, current, lag_rows, weight_scale)[:, pair_order].astype(
            jnp.bfloat16
        )
        own_piece = lax.psum_scatter(day_partial, "day", scatter_dimension=1, tiled=True).astype(
            jnp.float32
        )
        result = lax.dynamic_update_index_in_dim(result, own_piece, slot_index, 0)
        return (current, result)

    out_type = jnp.float32
    initial = (own_spectra, jnp.zeros((round_count, LAGS, share_width), out_type))
    current, result = lax.fori_loop(0, round_count, round_body, initial)
    return result


def solution(mesh):
    in_specs = (P("stn", "day", None), P(), P())
    out_specs = P(None, None, ("stn", "day"))
    return jax.shard_map(shards, mesh=mesh, in_specs=in_specs, out_specs=out_specs, check_vma=False)
```

profile of v0, /device:TPU:1, one launch (start us, length us, event | category | flops | bytes accessed | tf_op | source)
XLA Modules:
  0.0 1544.6 jit_solution(16583669919254134429)
XLA Ops:
  6.5 14.9 cosine_convert_fusion
  28.6 1509.4 %while.18 = (s32[]{:T(128)}, bf16[32,16,128]{0,1,2:T(8,128)(2,1)S(1)}, f32[16,101,64]{1,2,0:T(8,128)}, bf16[32,16,128]{0,1,2:T(8,128)(2,1)S(1)}, bf16[32,16,128]...) while((s32[]{:T(128)}, ...), condition=%wide.region_6.7_spmd.clone, body=%wide.region_3.6_spmd.clone.sunk | while | flops 61821300 | bytes 7378987 | solution.py:85
  28.6 5.5 collective-permute-start
  34.1 20.5 %collective-permute-done = bf16[32,16,128]{0,1,2:T(8,128)(2,1)S(1)} collective-permute-done((bf16[32,16,128]{0,1,2:T(8,128)(2,1)S(1)}, bf16[32,16,128]{0,1,2:T(8,128)(2,1)S(1)}, u32[]{:S(2)}, u32[]{:S(2)}) %collective-permute-start) | collective-permute-done | bytes 131104 | tf_op jit(solution)/shard_map/while/body/eval_jaxpr/ppermute | solution.py:17
  59.2 4.3 gather_fusion
  66.1 59.6 %reduce-scatter.2.cloned.1.call-done = bf16[101,64]{0,1:T(8,128)(2,1)} async-done(((bf16[101,1024]{0,1:T(8,128)(2,1)}), bf16[101,64]{0,1:T(8,128)(2,1)}) %reduce-scatter.2.cloned.1.call-update) | async-done | bytes 12944 | tf_op jit(solution)/shard_map/while/body/eval_jaxpr/reduce_scatter | solution.py:77
  130.7 12.0 collective-permute-done
  147.3 4.3 gather_fusion
  154.2 65.8 %reduce-scatter.2.cloned.1.call-done = bf16[101,64]{0,1:T(8,128)(2,1)} async-done(((bf16[101,1024]{0,1:T(8,128)(2,1)}), bf16[101,64]{0,1:T(8,128)(2,1)}) %reduce-scatter.2.cloned.1.call-update) | async-done | bytes 12944 | tf_op jit(solution)/shard_map/while/body/eval_jaxpr/reduce_scatter | solution.py:77
  225.0 11.8 collective-permute-done
  241.3 4.3 gather_fusion
  248.2 65.9 %reduce-scatter.2.cloned.1.call-done = bf16[101,64]{0,1:T(8,128)(2,1)} async-done(((bf16[101,1024]{0,1:T(8,128)(2,1)}), bf16[101,64]{0,1:T(8,128)(2,1)}) %reduce-scatter.2.cloned.1.call-update) | async-done | bytes 12944 | tf_op jit(solution)/shard_map/while/body/eval_jaxpr/reduce_scatter | solution.py:77
  319.1 11.8 collective-permute-done
  335.4 4.3 gather_fusion
  342.3 65.7 %reduce-scatter.2.cloned.1.call-done = bf16[101,64]{0,1:T(8,128)(2,1)} async-done(((bf16[101,1024]{0,1:T(8,128)(2,1)}), bf16[101,64]{0,1:T(8,128)(2,1)}) %reduce-scatter.2.cloned.1.call-update) | async-done | bytes 12944 | tf_op jit(solution)/shard_map/while/body/eval_jaxpr/reduce_scatter | solution.py:77
  413.1 11.8 collective-permute-done
  429.4 4.3 gather_fusion
  436.3 65.9 %reduce-scatter.2.cloned.1.call-done = bf16[101,64]{0,1:T(8,128)(2,1)} async-done(((bf16[101,1024]{0,1:T(8,128)(2,1)}), bf16[101,64]{0,1:T(8,128)(2,1)}) %reduce-scatter.2.cloned.1.call-update) | async-done | bytes 12944 | tf_op jit(solution)/shard_map/while/body/eval_jaxpr/reduce_scatter | solution.py:77
  507.0 12.0 collective-permute-done
  523.5 4.3 gather_fusion
  530.4 65.9 %reduce-scatter.2.cloned.1.call-done = bf16[101,64]{0,1:T(8,128)(2,1)} async-done(((bf16[101,1024]{0,1:T(8,128)(2,1)}), bf16[101,64]{0,1:T(8,128)(2,1)}) %reduce-scatter.2.cloned.1.call-update) | async-done | bytes 12944 | tf_op jit(solution)/shard_map/while/body/eval_jaxpr/reduce_scatter | solution.py:77
  601.1 11.9 collective-permute-done
  617.5 4.3 gather_fusion
  624.5 65.9 %reduce-scatter.2.cloned.1.call-done = bf16[101,64]{0,1:T(8,128)(2,1)} async-done(((bf16[101,1024]{0,1:T(8,128)(2,1)}), bf16[101,64]{0,1:T(8,128)(2,1)}) %reduce-scatter.2.cloned.1.call-update) | async-done | bytes 12944 | tf_op jit(solution)/shard_map/while/body/eval_jaxpr/reduce_scatter | solution.py:77
  695.2 11.9 collective-permute-done
  711.7 4.3 gather_fusion
  718.6 65.7 %reduce-scatter.2.cloned.1.call-done = bf16[101,64]{0,1:T(8,128)(2,1)} async-done(((bf16[101,1024]{0,1:T(8,128)(2,1)}), bf16[101,64]{0,1:T(8,128)(2,1)}) %reduce-scatter.2.cloned.1.call-update) | async-done | bytes 12944 | tf_op jit(solution)/shard_map/while/body/eval_jaxpr/reduce_scatter | solution.py:77
  789.4 11.8 collective-permute-done
  805.8 4.3 gather_fusion
  812.7 65.8 %reduce-scatter.2.cloned.1.call-done = bf16[101,64]{0,1:T(8,128)(2,1)} async-done(((bf16[101,1024]{0,1:T(8,128)(2,1)}), bf16[101,64]{0,1:T(8,128)(2,1)}) %reduce-scatter.2.cloned.1.call-update) | async-done | bytes 12944 | tf_op jit(solution)/shard_map/while/body/eval_jaxpr/reduce_scatter | solution.py:77
  883.5 11.7 collective-permute-done
  899.7 4.3 gather_fusion
  906.6 65.8 %reduce-scatter.2.cloned.1.call-done = bf16[101,64]{0,1:T(8,128)(2,1)} async-done(((bf16[101,1024]{0,1:T(8,128)(2,1)}), bf16[101,64]{0,1:T(8,128)(2,1)}) %reduce-scatter.2.cloned.1.call-update) | async-done | bytes 12944 | tf_op jit(solution)/shard_map/while/body/eval_jaxpr/reduce_scatter | solution.py:77
  977.5 11.8 collective-permute-done
  1000.8 65.7 %reduce-scatter.2.cloned.1.call-done = bf16[101,64]{0,1:T(8,128)(2,1)} async-done(((bf16[101,1024]{0,1:T(8,128)(2,1)}), bf16[101,64]{0,1:T(8,128)(2,1)}) %reduce-scatter.2.cloned.1.call-update) | async-done | bytes 12944 | tf_op jit(solution)/shard_map/while/body/eval_jaxpr/reduce_scatter | solution.py:77
  1071.4 11.9 collective-permute-done
  1087.9 4.3 gather_fusion
  1094.8 65.8 %reduce-scatter.2.cloned.1.call-done = bf16[101,64]{0,1:T(8,128)(2,1)} async-done(((bf16[101,1024]{0,1:T(8,128)(2,1)}), bf16[101,64]{0,1:T(8,128)(2,1)}) %reduce-scatter.2.cloned.1.call-update) | async-done | bytes 12944 | tf_op jit(solution)/shard_map/while/body/eval_jaxpr/reduce_scatter | solution.py:77
  1165.7 11.7 collective-permute-done
  1181.9 4.3 gather_fusion
  1188.8 65.9 %reduce-scatter.2.cloned.1.call-done = bf16[101,64]{0,1:T(8,128)(2,1)} async-done(((bf16[101,1024]{0,1:T(8,128)(2,1)}), bf16[101,64]{0,1:T(8,128)(2,1)}) %reduce-scatter.2.cloned.1.call-update) | async-done | bytes 12944 | tf_op jit(solution)/shard_map/while/body/eval_jaxpr/reduce_scatter | solution.py:77
  1259.6 11.9 collective-permute-done
  1276.0 4.3 gather_fusion
  1282.9 65.9 %reduce-scatter.2.cloned.1.call-done = bf16[101,64]{0,1:T(8,128)(2,1)} async-done(((bf16[101,1024]{0,1:T(8,128)(2,1)}), bf16[101,64]{0,1:T(8,128)(2,1)}) %reduce-scatter.2.cloned.1.call-update) | async-done | bytes 12944 | tf_op jit(solution)/shard_map/while/body/eval_jaxpr/reduce_scatter | solution.py:77
  1353.8 11.8 collective-permute-done
  1376.9 65.9 %reduce-scatter.2.cloned.1.call-done = bf16[101,64]{0,1:T(8,128)(2,1)} async-done(((bf16[101,1024]{0,1:T(8,128)(2,1)}), bf16[101,64]{0,1:T(8,128)(2,1)}) %reduce-scatter.2.cloned.1.call-update) | async-done | bytes 12944 | tf_op jit(solution)/shard_map/while/body/eval_jaxpr/reduce_scatter | solution.py:77
  1447.8 11.7 collective-permute-done
  1471.0 65.7 %reduce-scatter.2.cloned.1.call-done = bf16[101,64]{0,1:T(8,128)(2,1)} async-done(((bf16[101,1024]{0,1:T(8,128)(2,1)}), bf16[101,64]{0,1:T(8,128)(2,1)}) %reduce-scatter.2.cloned.1.call-update) | async-done | bytes 12944 | tf_op jit(solution)/shard_map/while/body/eval_jaxpr/reduce_scatter | solution.py:77
  (284 shorter events, 178.3 us)
Async XLA Ops:
  6.5 15.0 copy-start
  26.1 2.5 copy-start.1
  26.1 2.5 copy-start.2
  28.6 97.1 %reduce-scatter.2.cloned.1.call-start = ((), (), s32[]{:S(2)}) async-start(), calls=%async_computation.1 | async-start | bytes 278528 | tf_op jit(solution)/shard_map/while/body/eval_jaxpr/reduce_scatter | solution.py:77
  28.6 26.1 %collective-permute-start = (bf16[32,16,128]{0,1,2:T(8,128)(2,1)S(1)}, bf16[32,16,128]{0,1,2:T(8,128)(2,1)S(1)}, u32[]{:S(2)}, u32[]{:S(2)}) collective-permute-start(bf16[32,16,128]{0,1,2:T(8,128)(2,1)S(1)} %get-tuple-element.337), channel_id=1, source_target_pairs={{0,16},{16,32},{32,48},{48,64},{64,80},{80,96},{96,112},{112,128},... | collective-permute-start | bytes 393224 | tf_op jit(solution)/shard_map/while/body/eval_jaxpr/ppermute | solution.py:17
  127.1 92.9 %reduce-scatter.2.cloned.1.call-start = ((), (), s32[]{:S(2)}) async-start(), calls=%async_computation.1 | async-start | bytes 278528 | tf_op jit(solution)/shard_map/while/body/eval_jaxpr/reduce_scatter | solution.py:77
  127.1 15.7 %collective-permute-start = (bf16[32,16,128]{0,1,2:T(8,128)(2,1)S(1)}, bf16[32,16,128]{0,1,2:T(8,128)(2,1)S(1)}, u32[]{:S(2)}, u32[]{:S(2)}) collective-permute-start(bf16[32,16,128]{0,1,2:T(8,128)(2,1)S(1)} %get-tuple-element.337), channel_id=1, source_target_pairs={{0,16},{16,32},{32,48},{48,64},{64,80},{80,96},{96,112},{112,128},... | collective-permute-start | bytes 393224 | tf_op jit(solution)/shard_map/while/body/eval_jaxpr/ppermute | solution.py:17
  221.3 92.8 %reduce-scatter.2.cloned.1.call-start = ((), (), s32[]{:S(2)}) async-start(), calls=%async_computation.1 | async-start | bytes 278528 | tf_op jit(solution)/shard_map/while/body/eval_jaxpr/reduce_scatter | solution.py:77
  221.3 15.5 %collective-permute-start = (bf16[32,16,128]{0,1,2:T(8,128)(2,1)S(1)}, bf16[32,16,128]{0,1,2:T(8,128)(2,1)S(1)}, u32[]{:S(2)}, u32[]{:S(2)}) collective-permute-start(bf16[32,16,128]{0,1,2:T(8,128)(2,1)S(1)} %get-tuple-element.337), channel_id=1, source_target_pairs={{0,16},{16,32},{32,48},{48,64},{64,80},{80,96},{96,112},{112,128},... | collective-permute-start | bytes 393224 | tf_op jit(solution)/shard_map/while/body/eval_jaxpr/ppermute | solution.py:17
  315.4 92.5 %reduce-scatter.2.cloned.1.call-start = ((), (), s32[]{:S(2)}) async-start(), calls=%async_computation.1 | async-start | bytes 278528 | tf_op jit(solution)/shard_map/while/body/eval_jaxpr/reduce_scatter | solution.py:77
  315.5 15.4 collective-permute-start
  409.3 92.9 %reduce-scatter.2.cloned.1.call-start = ((), (), s32[]{:S(2)}) async-start(), calls=%async_computation.1 | async-start | bytes 278528 | tf_op jit(solution)/shard_map/while/body/eval_jaxpr/reduce_scatter | solution.py:77
  409.3 15.6 %collective-permute-start = (bf16[32,16,128]{0,1,2:T(8,128)(2,1)S(1)}, bf16[32,16,128]{0,1,2:T(8,128)(2,1)S(1)}, u32[]{:S(2)}, u32[]{:S(2)}) collective-permute-start(bf16[32,16,128]{0,1,2:T(8,128)(2,1)S(1)} %get-tuple-element.337), channel_id=1, source_target_pairs={{0,16},{16,32},{32,48},{48,64},{64,80},{80,96},{96,112},{112,128},... | collective-permute-start | bytes 393224 | tf_op jit(solution)/shard_map/while/body/eval_jaxpr/ppermute | solution.py:17
  503.6 92.7 %reduce-scatter.2.cloned.1.call-start = ((), (), s32[]{:S(2)}) async-start(), calls=%async_computation.1 | async-start | bytes 278528 | tf_op jit(solution)/shard_map/while/body/eval_jaxpr/reduce_scatter | solution.py:77
  503.6 15.4 collective-permute-start
  597.6 92.8 %reduce-scatter.2.cloned.1.call-start = ((), (), s32[]{:S(2)}) async-start(), calls=%async_computation.1 | async-start | bytes 278528 | tf_op jit(solution)/shard_map/while/body/eval_jaxpr/reduce_scatter | solution.py:77
  597.6 15.4 collective-permute-start
  691.7 92.5 %reduce-scatter.2.cloned.1.call-start = ((), (), s32[]{:S(2)}) async-start(), calls=%async_computation.1 | async-start | bytes 278528 | tf_op jit(solution)/shard_map/while/body/eval_jaxpr/reduce_scatter | solution.py:77
  691.7 15.4 collective-permute-start
  785.6 92.9 %reduce-scatter.2.cloned.1.call-start = ((), (), s32[]{:S(2)}) async-start(), calls=%async_computation.1 | async-start | bytes 278528 | tf_op jit(solution)/shard_map/while/body/eval_jaxpr/reduce_scatter | solution.py:77
  785.6 15.6 %collective-permute-start = (bf16[32,16,128]{0,1,2:T(8,128)(2,1)S(1)}, bf16[32,16,128]{0,1,2:T(8,128)(2,1)S(1)}, u32[]{:S(2)}, u32[]{:S(2)}) collective-permute-start(bf16[32,16,128]{0,1,2:T(8,128)(2,1)S(1)} %get-tuple-element.337), channel_id=1, source_target_pairs={{0,16},{16,32},{32,48},{48,64},{64,80},{80,96},{96,112},{112,128},... | collective-permute-start | bytes 393224 | tf_op jit(solution)/shard_map/while/body/eval_jaxpr/ppermute | solution.py:17
  879.8 92.5 %reduce-scatter.2.cloned.1.call-start = ((), (), s32[]{:S(2)}) async-start(), calls=%async_computation.1 | async-start | bytes 278528 | tf_op jit(solution)/shard_map/while/body/eval_jaxpr/reduce_scatter | solution.py:77
  879.8 15.3 collective-permute-start
  973.7 92.8 %reduce-scatter.2.cloned.1.call-start = ((), (), s32[]{:S(2)}) async-start(), calls=%async_computation.1 | async-start | bytes 278528 | tf_op jit(solution)/shard_map/while/body/eval_jaxpr/reduce_scatter | solution.py:77
  973.7 15.6 %collective-permute-start = (bf16[32,16,128]{0,1,2:T(8,128)(2,1)S(1)}, bf16[32,16,128]{0,1,2:T(8,128)(2,1)S(1)}, u32[]{:S(2)}, u32[]{:S(2)}) collective-permute-start(bf16[32,16,128]{0,1,2:T(8,128)(2,1)S(1)} %get-tuple-element.337), channel_id=1, source_target_pairs={{0,16},{16,32},{32,48},{48,64},{64,80},{80,96},{96,112},{112,128},... | collective-permute-start | bytes 393224 | tf_op jit(solution)/shard_map/while/body/eval_jaxpr/ppermute | solution.py:17
  1067.8 92.9 %reduce-scatter.2.cloned.1.call-start = ((), (), s32[]{:S(2)}) async-start(), calls=%async_computation.1 | async-start | bytes 278528 | tf_op jit(solution)/shard_map/while/body/eval_jaxpr/reduce_scatter | solution.py:77
  1067.8 15.6 %collective-permute-start = (bf16[32,16,128]{0,1,2:T(8,128)(2,1)S(1)}, bf16[32,16,128]{0,1,2:T(8,128)(2,1)S(1)}, u32[]{:S(2)}, u32[]{:S(2)}) collective-permute-start(bf16[32,16,128]{0,1,2:T(8,128)(2,1)S(1)} %get-tuple-element.337), channel_id=1, source_target_pairs={{0,16},{16,32},{32,48},{48,64},{64,80},{80,96},{96,112},{112,128},... | collective-permute-start | bytes 393224 | tf_op jit(solution)/shard_map/while/body/eval_jaxpr/ppermute | solution.py:17
  1162.0 92.8 %reduce-scatter.2.cloned.1.call-start = ((), (), s32[]{:S(2)}) async-start(), calls=%async_computation.1 | async-start | bytes 278528 | tf_op jit(solution)/shard_map/while/body/eval_jaxpr/reduce_scatter | solution.py:77
  1162.0 15.4 collective-permute-start
  1256.1 92.7 %reduce-scatter.2.cloned.1.call-start = ((), (), s32[]{:S(2)}) async-start(), calls=%async_computation.1 | async-start | bytes 278528 | tf_op jit(solution)/shard_map/while/body/eval_jaxpr/reduce_scatter | solution.py:77
  1256.1 15.4 collective-permute-start
  1350.1 92.8 %reduce-scatter.2.cloned.1.call-start = ((), (), s32[]{:S(2)}) async-start(), calls=%async_computation.1 | async-start | bytes 278528 | tf_op jit(solution)/shard_map/while/body/eval_jaxpr/reduce_scatter | solution.py:77
  1350.1 15.4 collective-permute-start
  1444.2 92.5 %reduce-scatter.2.cloned.1.call-start = ((), (), s32[]{:S(2)}) async-start(), calls=%async_computation.1 | async-start | bytes 278528 | tf_op jit(solution)/shard_map/while/body/eval_jaxpr/reduce_scatter | solution.py:77
  1444.2 15.4 collective-permute-start
Sparse Core Ops, SparseCore 0:
  63.6 62.0 reduce-scatter.1
  151.7 68.2 reduce-scatter.1
  245.7 68.3 reduce-scatter.1
  339.8 68.1 reduce-scatter.1
  433.8 68.3 reduce-scatter.1
  527.9 68.3 reduce-scatter.1
  622.0 68.3 reduce-scatter.1
  716.1 68.1 reduce-scatter.1
  810.2 68.2 reduce-scatter.1
  904.1 68.2 reduce-scatter.1
  998.3 68.1 reduce-scatter.1
  1092.3 68.2 reduce-scatter.1
  1186.3 68.3 reduce-scatter.1
  1280.4 68.3 reduce-scatter.1
  1374.5 68.3 reduce-scatter.1
  1468.5 68.1 reduce-scatter.1
where the time goes:
time: 1550 us; the launch traced here: 1540 us
  waiting for transfers between devices  1250 us (81%)
  local copies, waits for them, and re-layouts  121 us (8%)
  starting transfers between devices  59.4 us (4%)
  other arithmetic  49.7 us (3%)
  loops' own time  32 us (2%)
  matrix products  24.4 us (2%)
    reduce_scatter x16, waiting for transfers between devices, round_body(): lax.psum_scatter(day_partial, 'day', scatter_dimension=1, tiled=True)  1050 us
    ppermute x16, waiting for transfers between devices, from_behind(): return lax.ppermute(value, axis, pairs)  198 us
    gather x16, local copies, waits for them, and re-layouts, round_body(): correlate(own_spectra, current, lag_rows, weight_scale)[:, pair_order]  68.4 us
    ppermute x16, starting transfers between devices, from_behind(): return lax.ppermute(value, axis, pairs)  59.3 us
    another operation x1, loops' own time, shards(): current, result = lax.fori_loop(0, round_count, round_body, initial)  32 us
  transfers between devices with their start and end apart: 32, of which 32 were waited for; matrix products, arithmetic and copies ran while one was open for 1% of the time, Pallas kernels for 0%

commit v1 on v0

v1 whole, which is shorter than its diff:
```python
import functools
import math

import jax
import jax.numpy as jnp
import ml_dtypes
import numpy as np
from jax import lax
from jax.experimental import pallas as pl
from jax.experimental.pallas import tpu as pltpu
from jax.sharding import Mesh
from jax.sharding import PartitionSpec as P

SB = 32
DD = 8
NT = 6000
NB = 128
K0 = 30
LAGS = 101
ROUNDS = 16
N_DAY = 16
N_HI = 2
ZG = 4
NBLK = ZG * N_HI
GROUP = NBLK * N_DAY
BACK = ROUNDS // NBLK
SEEN = ROUNDS + NBLK
KDIM = DD * N_DAY * 2
PAIRS = SB * SB
SHARE = PAIRS // N_DAY
LAG_ROWS = 104
HALF = SB // 2
VMEM = 44 * 1024 * 1024

assert NB == GROUP


def phase_table(columns):
    bins = np.arange(NB, dtype=np.int64) + K0
    turns = (bins[:, None] * columns[None, :]) % NT
    angle = 2.0 * math.pi / NT * turns.astype(np.float64)
    return np.cos(angle).astype(ml_dtypes.bfloat16), (-np.sin(angle)).astype(ml_dtypes.bfloat16)


def band_table():
    real, imag = phase_table(np.arange(NT, dtype=np.int64))
    return np.stack([real, imag], axis=1).reshape(2 * NB, NT)


def lag_table():
    real, imag = phase_table(np.arange(LAGS, dtype=np.int64) - LAGS // 2)
    table = np.zeros((LAG_ROWS, 2 * NB), ml_dtypes.bfloat16)
    table[:LAGS, :NB] = real.T
    table[:LAGS, NB:] = imag.T
    return table


def day_major():
    table = np.zeros((HALF * DD, HALF * DD), ml_dtypes.bfloat16)
    for s in range(HALF):
        for e in range(DD):
            table[s * DD + e, e * HALF + s] = 1
    return table


def spread_rows():
    table = np.zeros((2 * NBLK * SB, NBLK * SB), ml_dtypes.bfloat16)
    for i in range(SB):
        for c in range(2):
            for b in range(NBLK):
                table[i * 2 * NBLK + c * NBLK + b, b * SB + i] = 1
    return table


def pick_rows():
    half = ROUNDS // 2
    table = np.zeros((2 * NBLK * ROUNDS, SEEN * 2 * NBLK), ml_dtypes.bfloat16)
    for h in range(2):
        for b in range(NBLK):
            for s in range(half):
                for c in range(2):
                    met = b + ROUNDS - (h * half + s + 1)
                    row = ((h * NBLK + b) * half + s) * 2 + c
                    table[row, met * 2 * NBLK + c * NBLK + b] = 1
    return table


def spectra_kernel(x_ref, band_ref, order_ref, out_ref):
    x = x_ref[...].astype(jnp.float32).reshape(HALF * DD, NT)
    x = x - jnp.sum(x, axis=1, keepdims=True) * (1.0 / NT)
    power = jnp.sum(x * x, axis=1, keepdims=True) * (1.0 / NT)
    x = (x / jnp.sqrt(power + 1e-06)).astype(jnp.bfloat16)
    raw = lax.dot_general(
        band_ref[...], x, (((1,), (1,)), ((), ())), preferred_element_type=jnp.float32
    )
    scale = jnp.sqrt(jnp.sum(raw * raw, axis=0, keepdims=True) * (1.0 / NB) + 1e-06)
    spectra = (raw / scale).astype(jnp.bfloat16)
    out_ref[...] = jnp.dot(
        spectra, order_ref[...], preferred_element_type=jnp.float32
    ).astype(jnp.bfloat16)


def gather_days_kernel(r_ref, out_ref, wide_ref):
    turned = r_ref[...].astype(jnp.float32).T
    width = 2 * N_DAY
    for half in range(2):
        for e in range(DD):
            row = half * HALF * DD + e * HALF
            for b in range(NBLK):
                wide_ref[b * SB + half * HALF : b * SB + (half + 1) * HALF,
                         e * width : (e + 1) * width] = (
                    turned[row : row + HALF, b * width : (b + 1) * width]
                )
    out_ref[...] = wide_ref[...].astype(jnp.bfloat16)


def cross_kernel(*refs):
    met_refs = refs[: BACK + 1]
    spread_ref, pick_ref, choice_ref, out_ref, cross_ref, pair_ref = refs[BACK + 1 :]
    own = met_refs[0][...]
    wide = own.astype(jnp.float32)
    lane = lax.broadcasted_iota(jnp.int32, wide.shape, 1)
    turned = jnp.where(
        lane % 2 == 0, pltpu.roll(wide, KDIM - 1, 1), -pltpu.roll(wide, 1, 1)
    ).astype(jnp.bfloat16)
    spread = spread_ref[...]
    rows = lax.broadcasted_iota(jnp.int32, (2 * NBLK * SB, KDIM), 0)
    left = jnp.where(
        rows % (2 * NBLK) < NBLK,
        jnp.dot(spread, own, preferred_element_type=jnp.float32),
        jnp.dot(spread, turned, preferred_element_type=jnp.float32),
    ).astype(jnp.bfloat16)
    for step in range(BACK + 1):
        start = (BACK - step) * NBLK * SB
        cross_ref[:, start : start + NBLK * SB] = lax.dot_general(
            left, met_refs[step][...], (((1,), (1,)), ((), ())),
            preferred_element_type=jnp.float32,
        )
    for i in range(SB):
        piece = cross_ref[i * 2 * NBLK : (i + 1) * 2 * NBLK, :]
        for met in range(SEEN):
            pair_ref[met * 2 * NBLK : (met + 1) * 2 * NBLK, i * SB : (i + 1) * SB] = (
                piece[:, met * SB : (met + 1) * SB]
            )
    picked = jnp.dot(
        pick_ref[...], pair_ref[...].astype(jnp.bfloat16), preferred_element_type=jnp.float32
    ).astype(jnp.bfloat16)
    chosen = jnp.dot(picked, choice_ref[...], preferred_element_type=jnp.float32)
    height = ROUNDS
    first = lax.broadcasted_iota(jnp.int32, (height, 2 * SHARE), 1) < SHARE
    for b in range(NBLK):
        for d in range(0, N_DAY, 2):
            low = chosen[b * height : (b + 1) * height, d * SHARE : (d + 2) * SHARE]
            high = chosen[
                (NBLK + b) * height : (NBLK + b + 1) * height, d * SHARE : (d + 2) * SHARE
            ]
            even = jnp.where(first, low, pltpu.roll(high, SHARE, 1))
            odd = jnp.where(first, pltpu.roll(low, SHARE, 1), high)
            out_ref[b * N_DAY + d] = even.astype(jnp.bfloat16)
            out_ref[b * N_DAY + d + 1] = odd.astype(jnp.bfloat16)


def lag_kernel(slot_ref, r_ref, lag_ref, out_ref, wide_ref):
    height = ROUNDS
    half = ROUNDS // 2
    wide_ref[...] = r_ref[...].astype(jnp.float32).reshape(GROUP * height, 2 * SHARE)
    lag = lag_ref[...]
    for s in range(half):
        real = wide_ref[pl.ds(2 * s, GROUP, stride=height), :].astype(jnp.bfloat16)
        imag = wide_ref[pl.ds(2 * s + 1, GROUP, stride=height), :].astype(jnp.bfloat16)
        lagged = jnp.dot(lag[:, :NB], real, preferred_element_type=jnp.float32)
        lagged = lagged + jnp.dot(lag[:, NB:], imag, preferred_element_type=jnp.float32)
        lagged = lagged * (1.0 / math.sqrt(NB * DD * N_DAY))
        out_ref[slot_ref[s]] = lagged[:LAGS, :SHARE]
        out_ref[slot_ref[half + s]] = lagged[:LAGS, SHARE:]


def params():
    return pltpu.CompilerParams(vmem_limit_bytes=VMEM)


def vmem_specs(count):
    return [pl.BlockSpec(memory_space=pltpu.VMEM)] * count


def shards(records, offsets, pair_order):
    group_axes = ("zr", "xh", "day")
    spectra = pl.pallas_call(
        spectra_kernel,
        grid=(2,),
        in_specs=[
            pl.BlockSpec((HALF, DD, NT), lambda i: (i, 0, 0)),
            pl.BlockSpec((2 * NB, NT), lambda i: (0, 0)),
            pl.BlockSpec((HALF * DD, HALF * DD), lambda i: (0, 0)),
        ],
        out_specs=pl.BlockSpec((2 * NB, HALF * DD), lambda i: (0, i)),
        out_shape=jax.ShapeDtypeStruct((2 * NB, SB * DD), jnp.bfloat16),
        compiler_params=params(),
        name="spectra",
    )(records, jnp.asarray(band_table()), jnp.asarray(day_major()))

    by_bin = lax.all_to_all(
        spectra.reshape(GROUP, 2, SB * DD), group_axes, 0, 0, tiled=True
    ).reshape(2 * NB, SB * DD)

    own = pl.pallas_call(
        gather_days_kernel,
        in_specs=vmem_specs(1),
        out_specs=pl.BlockSpec(memory_space=pltpu.VMEM),
        out_shape=jax.ShapeDtypeStruct((NBLK * SB, KDIM), jnp.bfloat16),
        scratch_shapes=[pltpu.VMEM((NBLK * SB, KDIM), jnp.float32)],
        compiler_params=params(),
        name="gather_days",
    )(by_bin)

    groups = lax.axis_size("zq")
    pairs = [(source, (source + 1) % groups) for source in range(groups)]
    met = [own]
    for _ in range(BACK):
        met.append(lax.ppermute(met[-1], "zq", pairs))

    choice = (
        lax.broadcasted_iota(jnp.int32, (PAIRS, PAIRS), 0) == pair_order[None, :]
    ).astype(jnp.bfloat16)

    chosen = pl.pallas_call(
        cross_kernel,
        in_specs=vmem_specs(BACK + 4),
        out_specs=pl.BlockSpec(memory_space=pltpu.VMEM),
        out_shape=jax.ShapeDtypeStruct((GROUP, ROUNDS, 2 * SHARE), jnp.bfloat16),
        scratch_shapes=[
            pltpu.VMEM((2 * NBLK * SB, SEEN * SB), jnp.float32),
            pltpu.VMEM((2 * NBLK * SEEN, PAIRS), jnp.float32),
        ],
        compiler_params=params(),
        name="cross",
    )(*met, jnp.asarray(spread_rows()), jnp.asarray(pick_rows()), choice)

    by_pair = lax.all_to_all(chosen, group_axes, 0, 0, tiled=True)

    steps = jnp.arange(ROUNDS, dtype=jnp.int32)
    slots = jnp.sum(
        jnp.where(offsets[None, :] == steps[:, None], steps[None, :], 0), axis=1
    ).astype(jnp.int32)

    return pl.pallas_call(
        lag_kernel,
        in_specs=[pl.BlockSpec(memory_space=pltpu.SMEM)] + vmem_specs(2),
        out_specs=pl.BlockSpec(memory_space=pltpu.VMEM),
        out_shape=jax.ShapeDtypeStruct((ROUNDS, LAGS, SHARE), jnp.float32),
        scratch_shapes=[pltpu.VMEM((GROUP * ROUNDS, 2 * SHARE), jnp.float32)],
        compiler_params=params(),
        name="lags",
    )(slots, by_pair, jnp.asarray(lag_table()))


def solution(mesh):
    planes = mesh.shape["stn"] // N_HI
    devices = mesh.devices.reshape(planes // ZG, ZG, N_HI, mesh.shape["day"])
    fine = Mesh(devices, ("zq", "zr", "xh", "day"))
    stations = ("zq", "zr", "xh")
    in_specs = (P(stations, "day", None), P(), P())
    out_specs = P(None, None, stations + ("day",))
    return jax.shard_map(
        shards, mesh=fine, in_specs=in_specs, out_specs=out_specs, check_vma=False
    )
```

time: 1550 us -> 102 us (0.07)
  waiting for transfers between devices: 1250 us -> 27.4 us
  local copies, waits for them, and re-layouts: 121 us -> 5.73 us
  other arithmetic: 49.7 us -> 1 us
  loops' own time: 32 us -> 0 us
  starting transfers between devices: 59.4 us -> 33.5 us
  blocking collectives: 0 us -> 24.7 us
  matrix products: 24.4 us -> 0 us
    reduce_scatter x16 -> x0, waiting for transfers between devices: 1050 us -> none  [round_body(): lax.psum_scatter(day_partial, 'day', scatter_dimension=1, tiled=True)]
    ppermute x16 -> x2, waiting for transfers between devices: 198 us -> 9.25 us  [shards(): met.append(lax.ppermute(met[-1], 'zq', pairs))]
    gather x16 -> x0, local copies, waits for them, and re-layouts: 68.4 us -> none  [round_body(): correlate(own_spectra, current, lag_rows, weight_scale)[:, pair_order]]
    ppermute x16 -> x2, starting transfers between devices: 59.3 us -> 20.3 us  [shards(): met.append(lax.ppermute(met[-1], 'zq', pairs))]
    dot_general x32 -> x0, local copies, waits for them, and re-layouts: 38.1 us -> none  [the longest x16 20.8 us: correlate(): jnp.einsum('ick,jck->ijk', own_spectra, partner, preferred_element_type=j...]
    another operation x1 -> x0, loops' own time: 32 us -> none  [shards(): current, result = lax.fori_loop(0, round_count, round_body, initial)]
    all_to_all x0 -> x1, blocking collectives: none -> 24.7 us  [shards(): lax.all_to_all(spectra.reshape(GROUP, 2, SB * DD), group_axes, 0, 0, tile...]
    dot_general x49 -> x0, matrix products: 24.4 us -> none  [the longest x16 8.34 us: correlate(): jnp.einsum('ick,jck->ijk', own_spectra, partner, preferred_element_type=j...]
  transfers between devices with their start and end apart: 32 -> 3, of which waited for: 32 -> 3; matrix products, arithmetic and copies ran while one was open for 1% -> 1% of each run, Pallas kernels for 0% -> 0%
where the time goes in v1:
time: 102 us
  starting transfers between devices  33.5 us (33%)
  waiting for transfers between devices  27.4 us (27%)
  blocking collectives  24.7 us (24%)
  Pallas kernels  8.95 us (9%)
  local copies, waits for them, and re-layouts  5.73 us (6%)
    all_to_all x1, blocking collectives, shards(): lax.all_to_all(spectra.reshape(GROUP, 2, SB * DD), group_axes, 0, 0, tile...  24.7 us
    ppermute x2, starting transfers between devices, shards(): met.append(lax.ppermute(met[-1], 'zq', pairs))  20.3 us
    all_to_all x1, waiting for transfers between devices, shards(): by_pair = lax.all_to_all(chosen, group_axes, 0, 0, tiled=True)  18.2 us
    all_to_all x1, starting transfers between devices, shards(): by_pair = lax.all_to_all(chosen, group_axes, 0, 0, tiled=True)  13.2 us
    ppermute x2, waiting for transfers between devices, shards(): met.append(lax.ppermute(met[-1], 'zq', pairs))  9.25 us
    unnamed x16, local copies, waits for them, and re-layouts  4.53 us
    pallas_call x1, Pallas kernels, shards(): pl.pallas_call(spectra_kernel, grid=(2,), in_specs=[pl.BlockSpec((HALF, D...  3.95 us
    pallas_call x1, Pallas kernels, shards(): pl.pallas_call(cross_kernel, in_specs=vmem_specs(BACK + 4), out_specs=pl....  3.59 us
  transfers between devices with their start and end apart: 3, of which 3 were waited for; matrix products, arithmetic and copies ran while one was open for 1% of the time, Pallas kernels for 0%

profile of v1, /device:TPU:1, one launch (start us, length us, event | category | flops | bytes accessed | tf_op | source)
XLA Modules:
  0.0 101.5 jit_solution(12601917511896024356)
XLA Ops:
  0.0 0.0 copy-start
  0.0 1.9 %copy-done = bf16[32,8,6000]{2,1,0:T(8,128)(2,1)S(1)} copy-done((bf16[32,8,6000]{2,1,0:T(8,128)(2,1)S(1)}, bf16[32,8,6000]{2,1,0:T(8,128)(2,1)}, u32[]{:S(2)}) %copy-start) | copy-done | bytes 3072024
  1.9 0.0 copy-start.1
  1.9 1.9 %copy-done.1 = bf16[256,6000]{1,0:T(8,128)(2,1)S(1)} copy-done((bf16[256,6000]{1,0:T(8,128)(2,1)S(1)}, bf16[256,6000]{1,0:T(8,128)(2,1)}, u32[]{:S(2)}) %copy-start.1) | copy-done | bytes 3072024
  3.7 0.0 copy-start.5
  3.7 0.8 copy-done.5
  4.5 0.0 copy-start.6
  4.5 3.9 %spectra.1 = bf16[256,256]{1,0:T(8,128)(2,1)S(1)} custom-call(bf16[32,8,6000]{2,1,0:T(8,128)(2,1)S(1)} %copy-done, bf16[256,6000]{1,0:T(8,128)(2,1)S(1)} %copy-done.1, bf16[128,128]{1,0:T(8,128)(2,1)S(1)} %copy-done.5), custom_call_target="tpu_custom_call" | custom-call | tf_op jit(solution)/shard_map/spectra/pallas_call | solution.py:188
  8.5 0.0 copy-start.2
  8.5 0.0 copy-start.3
  8.5 0.1 reshape.8
  8.5 24.7 %all_to_all.10 = bf16[128,2,256]{2,1,0:T(2,128)(2,1)S(1)} all-to-all(bf16[128,2,256]{2,1,0:T(2,128)(2,1)S(1)} %reshape.8), channel_id=1, replica_groups=mesh['zq'=4,'zr'=4,'xh'=2,'day'=16] {'zr','xh','day'}, dimensions={0} | all-to-all | bytes 262144 | tf_op jit(solution)/shard_map/all_to_all | solution.py:202
  33.3 0.1 reshape.9.r_ref
  33.3 0.3 gather_days.1.refs_0_
  33.6 0.0 copy-start.7
  33.6 0.0 copy-start.4
  33.6 8.9 %collective-permute-start = (bf16[256,256]{1,0:T(8,128)(2,1)S(1)}, bf16[256,256]{1,0:T(8,128)(2,1)S(1)}, u32[]{:S(2)}, u32[]{:S(2)}) collective-permute-start(bf16[256,256]{1,0:T(8,128)(2,1)S(1)} %gather_days.1.refs_0_), channel_id=1, source_target_pairs={{0,128},{128,256},{256,384},{384,0},{1,129},{129,257},{257,385},{3... | collective-permute-start | bytes 393224 | tf_op jit(solution)/shard_map/ppermute | solution.py:220
  42.6 4.4 %collective-permute-done.refs_1_ = bf16[256,256]{1,0:T(8,128)(2,1)S(1)} collective-permute-done((bf16[256,256]{1,0:T(8,128)(2,1)S(1)}, bf16[256,256]{1,0:T(8,128)(2,1)S(1)}, u32[]{:S(2)}, u32[]{:S(2)}) %collective-permute-start) | collective-permute-done | bytes 131104 | tf_op jit(solution)/shard_map/ppermute | solution.py:220
  47.0 11.4 %collective-permute-start.1 = (bf16[256,256]{1,0:T(8,128)(2,1)S(1)}, bf16[256,256]{1,0:T(8,128)(2,1)S(1)}, u32[]{:S(2)}, u32[]{:S(2)}) collective-permute-start(bf16[256,256]{1,0:T(8,128)(2,1)S(1)} %collective-permute-done.refs_1_), channel_id=1, source_target_pairs={{0,128},{128,256},{256,384},{384,0},{1,129},{129,257},{257,385},{3... | collective-permute-start | bytes 393224 | tf_op jit(solution)/shard_map/ppermute | solution.py:220
  58.4 0.0 copy-done.6
  58.4 0.9 fusion.refs_5_
  59.3 4.9 %collective-permute-done.1.refs_2_ = bf16[256,256]{1,0:T(8,128)(2,1)S(1)} collective-permute-done((bf16[256,256]{1,0:T(8,128)(2,1)S(1)}, bf16[256,256]{1,0:T(8,128)(2,1)S(1)}, u32[]{:S(2)}, u32[]{:S(2)}) %collective-permute-start.1) | collective-permute-done | bytes 131104 | tf_op jit(solution)/shard_map/ppermute | solution.py:220
  64.1 0.0 copy-done.2
  64.1 0.0 copy-done.3
  64.1 3.6 %cross.1 = bf16[128,16,128]{2,1,0:T(8,128)(2,1)} custom-call(bf16[256,256]{1,0:T(8,128)(2,1)S(1)} %gather_days.1.refs_0_, bf16[256,256]{1,0:T(8,128)(2,1)S(1)} %collective-permute-done.refs_1_, bf16[256,256]{1,0:T(8,128)(2,1)S(1)} %collective-permute-done.1.refs_2_, bf16[512,256]{1,0:T(8,128)(2,1)S(1)} %copy-done.2, bf16[256,384]{1,0:T(8,128)(2,1)S(1)} %copy-done.3, ...), custom_call_target="tpu_custom_call" | custom-call | tf_op jit(solution)/shard_map/cross/pallas_call | solution.py:226
  67.7 13.2 %all-to-all-start.1 = ((bf16[128,16,128]{2,1,0:T(8,128)(2,1)}), bf16[128,16,128]{2,1,0:T(8,128)(2,1)S(1)}, u32[]{:S(2)}, u32[]{:S(2)}) async-start(bf16[128,16,128]{2,1,0:T(8,128)(2,1)} %cross.1), calls=%async_computation.1 | async-start | bytes 1048576 | tf_op jit(solution)/shard_map/all_to_all | solution.py:239
  80.9 0.0 copy-done.7
  80.9 0.1 select_reduce_fusion.slot_ref
  81.1 18.2 %all-to-all-done.1.r_ref = bf16[128,16,128]{2,1,0:T(8,128)(2,1)S(1)} async-done(((bf16[128,16,128]{2,1,0:T(8,128)(2,1)}), bf16[128,16,128]{2,1,0:T(8,128)(2,1)S(1)}, u32[]{:S(2)}, u32[]{:S(2)}) %all-to-all-start.1) | async-done | bytes 524320 | tf_op jit(solution)/shard_map/all_to_all | solution.py:239
  99.3 0.0 copy-done.4
  99.3 1.2 %lags.1 = f32[16,101,64]{2,1,0:T(8,128)S(1)} custom-call(s32[16]{0:T(128)S(1)} %select_reduce_fusion.slot_ref, bf16[128,16,128]{2,1,0:T(8,128)(2,1)S(1)} %all-to-all-done.1.r_ref, bf16[104,256]{1,0:T(8,128)(2,1)S(1)} %copy-done.4), custom_call_target="tpu_custom_call" | custom-call | tf_op jit(solution)/shard_map/lags/pallas_call | solution.py:246
  100.4 1.1 %copy.10 = f32[16,101,64]{1,2,0:T(8,128)} copy(f32[16,101,64]{2,1,0:T(8,128)S(1)} %lags.1) | data formatting | bytes 827392 | tf_op jit(solution)/shard_map/lags/pallas_call | solution.py:246
Async XLA Ops:
  0.0 1.9 %copy-start = (bf16[32,8,6000]{2,1,0:T(8,128)(2,1)S(1)}, bf16[32,8,6000]{2,1,0:T(8,128)(2,1)}, u32[]{:S(2)}) copy-start(bf16[32,8,6000]{2,1,0:T(8,128)(2,1)} %x_ref.1) | copy-start | bytes 9216004
  1.9 1.9 %copy-start.1 = (bf16[256,6000]{1,0:T(8,128)(2,1)S(1)}, bf16[256,6000]{1,0:T(8,128)(2,1)}, u32[]{:S(2)}) copy-start(bf16[256,6000]{1,0:T(8,128)(2,1)} %constant.12.clone.band_ref) | copy-start | bytes 9216004
  3.7 0.8 copy-start.5
  4.5 53.9 %copy-start.6 = (s32[1024]{0:T(1024)S(1)}, s32[1024]{0:T(1024)}, u32[]{:S(2)}) copy-start(s32[1024]{0:T(1024)} %param.10) | copy-start | bytes 12292
  8.5 55.7 %copy-start.2 = (bf16[512,256]{1,0:T(8,128)(2,1)S(1)}, bf16[512,256]{1,0:T(8,128)(2,1)}, u32[]{:S(2)}) copy-start(bf16[512,256]{1,0:T(8,128)(2,1)} %constant.14.clone.refs_3_) | copy-start | bytes 786436
  8.5 55.6 %copy-start.3 = (bf16[256,384]{1,0:T(8,128)(2,1)S(1)}, bf16[256,384]{1,0:T(8,128)(2,1)}, u32[]{:S(2)}) copy-start(bf16[256,384]{1,0:T(8,128)(2,1)} %constant.15.clone.refs_4_) | copy-start | bytes 589828
  33.6 47.3 %copy-start.7 = (s32[16]{0:T(128)S(1)}, s32[16]{0:T(128)}, u32[]{:S(2)}) copy-start(s32[16]{0:T(128)} %param.9) | copy-start | bytes 196
  33.6 65.6 %copy-start.4 = (bf16[104,256]{1,0:T(8,128)(2,1)S(1)}, bf16[104,256]{1,0:T(8,128)(2,1)}, u32[]{:S(2)}) copy-start(bf16[104,256]{1,0:T(8,128)(2,1)} %constant.16.clone.lag_ref) | copy-start | bytes 159748
  33.6 13.3 %collective-permute-start = (bf16[256,256]{1,0:T(8,128)(2,1)S(1)}, bf16[256,256]{1,0:T(8,128)(2,1)S(1)}, u32[]{:S(2)}, u32[]{:S(2)}) collective-permute-start(bf16[256,256]{1,0:T(8,128)(2,1)S(1)} %gather_days.1.refs_0_), channel_id=1, source_target_pairs={{0,128},{128,256},{256,384},{384,0},{1,129},{129,257},{257,385},{3... | collective-permute-start | bytes 393224 | tf_op jit(solution)/shard_map/ppermute | solution.py:220
  47.0 17.1 %collective-permute-start.1 = (bf16[256,256]{1,0:T(8,128)(2,1)S(1)}, bf16[256,256]{1,0:T(8,128)(2,1)S(1)}, u32[]{:S(2)}, u32[]{:S(2)}) collective-permute-start(bf16[256,256]{1,0:T(8,128)(2,1)S(1)} %collective-permute-done.refs_1_), channel_id=1, source_target_pairs={{0,128},{128,256},{256,384},{384,0},{1,129},{129,257},{257,385},{3... | collective-permute-start | bytes 393224 | tf_op jit(solution)/shard_map/ppermute | solution.py:220
  67.7 31.5 %all-to-all-start.1 = ((bf16[128,16,128]{2,1,0:T(8,128)(2,1)}), bf16[128,16,128]{2,1,0:T(8,128)(2,1)S(1)}, u32[]{:S(2)}, u32[]{:S(2)}) async-start(bf16[128,16,128]{2,1,0:T(8,128)(2,1)} %cross.1), calls=%async_computation.1 | async-start | bytes 1048576 | tf_op jit(solution)/shard_map/all_to_all | solution.py:239

commit v2 on v1

--- a/solution.py
+++ b/solution.py
@@ -20,19 +20,25 @@
 ROUNDS = 16
 N_DAY = 16
 N_HI = 2
-ZG = 4
+PLANES = 16
+ZG = 1
 NBLK = ZG * N_HI
 GROUP = NBLK * N_DAY
+KB = NB // GROUP
+ENT = 2 * KB
+MIX = ENT * NBLK
+GROUPS = PLANES // ZG
 BACK = ROUNDS // NBLK
 SEEN = ROUNDS + NBLK
-KDIM = DD * N_DAY * 2
+WIDTH = N_DAY * ENT
+KDIM = DD * WIDTH
 PAIRS = SB * SB
 SHARE = PAIRS // N_DAY
 LAG_ROWS = 104
 HALF = SB // 2
 VMEM = 44 * 1024 * 1024
 
-assert NB == GROUP
+assert NB == GROUP * KB and ROUNDS == BACK * NBLK
 
 
 def phase_table(columns):
@@ -44,14 +50,15 @@
 
 def band_table():
     real, imag = phase_table(np.arange(NT, dtype=np.int64))
-    return np.stack([real, imag], axis=1).reshape(2 * NB, NT)
+    rows = np.stack([real.reshape(GROUP, KB, NT), imag.reshape(GROUP, KB, NT)], axis=1)
+    return rows.reshape(2 * NB, NT)
 
 
 def lag_table():
     real, imag = phase_table(np.arange(LAGS, dtype=np.int64) - LAGS // 2)
     table = np.zeros((LAG_ROWS, 2 * NB), ml_dtypes.bfloat16)
-    table[:LAGS, :NB] = real.T
-    table[:LAGS, NB:] = imag.T
+    rows = np.stack([real.reshape(GROUP, KB, LAGS), imag.reshape(GROUP, KB, LAGS)], axis=0)
+    table[:LAGS] = rows.transpose(3, 0, 2, 1).reshape(LAGS, 2 * NB)
     return table
 
 
@@ -64,24 +71,24 @@
 
 
 def spread_rows():
-    table = np.zeros((2 * NBLK * SB, NBLK * SB), ml_dtypes.bfloat16)
+    table = np.zeros((MIX * SB, NBLK * SB), ml_dtypes.bfloat16)
     for i in range(SB):
-        for c in range(2):
+        for c in range(ENT):
             for b in range(NBLK):
-                table[i * 2 * NBLK + c * NBLK + b, b * SB + i] = 1
+                table[i * MIX + c * NBLK + b, b * SB + i] = 1
     return table
 
 
 def pick_rows():
     half = ROUNDS // 2
-    table = np.zeros((2 * NBLK * ROUNDS, SEEN * 2 * NBLK), ml_dtypes.bfloat16)
+    table = np.zeros((MIX * ROUNDS, SEEN * MIX), ml_dtypes.bfloat16)
     for h in range(2):
         for b in range(NBLK):
             for s in range(half):
-                for c in range(2):
+                for c in range(ENT):
                     met = b + ROUNDS - (h * half + s + 1)
-                    row = ((h * NBLK + b) * half + s) * 2 + c
-                    table[row, met * 2 * NBLK + c * NBLK + b] = 1
+                    row = ((h * NBLK + b) * half + s) * ENT + c
+                    table[row, met * MIX + c * NBLK + b] = 1
     return table
 
 
@@ -102,51 +109,53 @@
 
 def gather_days_kernel(r_ref, out_ref, wide_ref):
     turned = r_ref[...].astype(jnp.float32).T
-    width = 2 * N_DAY
     for half in range(2):
         for e in range(DD):
             row = half * HALF * DD + e * HALF
             for b in range(NBLK):
                 wide_ref[b * SB + half * HALF : b * SB + (half + 1) * HALF,
-                         e * width : (e + 1) * width] = (
-                    turned[row : row + HALF, b * width : (b + 1) * width]
+                         e * WIDTH : (e + 1) * WIDTH] = (
+                    turned[row : row + HALF, b * WIDTH : (b + 1) * WIDTH]
                 )
     out_ref[...] = wide_ref[...].astype(jnp.bfloat16)
 
 
-def cross_kernel(*refs):
-    met_refs = refs[: BACK + 1]
-    spread_ref, pick_ref, choice_ref, out_ref, cross_ref, pair_ref = refs[BACK + 1 :]
-    own = met_refs[0][...]
+def cross_kernel(
+    place_ref, own_ref, all_ref, spread_ref, pick_ref, choice_ref, out_ref, met_ref, cross_ref, pair_ref
+):
+    own = own_ref[...]
     wide = own.astype(jnp.float32)
     lane = lax.broadcasted_iota(jnp.int32, wide.shape, 1)
     turned = jnp.where(
-        lane % 2 == 0, pltpu.roll(wide, KDIM - 1, 1), -pltpu.roll(wide, 1, 1)
+        lane % ENT < KB, pltpu.roll(wide, KDIM - KB, 1), -pltpu.roll(wide, KB, 1)
     ).astype(jnp.bfloat16)
     spread = spread_ref[...]
-    rows = lax.broadcasted_iota(jnp.int32, (2 * NBLK * SB, KDIM), 0)
+    row = lax.broadcasted_iota(jnp.int32, (MIX * SB, KDIM), 0)
+    lane = lax.broadcasted_iota(jnp.int32, (MIX * SB, KDIM), 1)
     left = jnp.where(
-        rows % (2 * NBLK) < NBLK,
+        row % MIX < MIX // 2,
         jnp.dot(spread, own, preferred_element_type=jnp.float32),
         jnp.dot(spread, turned, preferred_element_type=jnp.float32),
-    ).astype(jnp.bfloat16)
+    )
+    left = jnp.where(row // NBLK % KB == lane % KB, left, 0.0).astype(jnp.bfloat16)
+    height = NBLK * SB
     for step in range(BACK + 1):
-        start = (BACK - step) * NBLK * SB
-        cross_ref[:, start : start + NBLK * SB] = lax.dot_general(
-            left, met_refs[step][...], (((1,), (1,)), ((), ())),
-            preferred_element_type=jnp.float32,
-        )
+        source = lax.rem(place_ref[0] + (GROUPS - BACK + step), GROUPS)
+        met_ref[step * height : (step + 1) * height, :] = all_ref[source]
+    cross_ref[...] = lax.dot_general(
+        left, met_ref[...], (((1,), (1,)), ((), ())), preferred_element_type=jnp.float32
+    )
     for i in range(SB):
-        piece = cross_ref[i * 2 * NBLK : (i + 1) * 2 * NBLK, :]
+        piece = cross_ref[i * MIX : (i + 1) * MIX, :]
         for met in range(SEEN):
-            pair_ref[met * 2 * NBLK : (met + 1) * 2 * NBLK, i * SB : (i + 1) * SB] = (
+            pair_ref[met * MIX : (met + 1) * MIX, i * SB : (i + 1) * SB] = (
                 piece[:, met * SB : (met + 1) * SB]
             )
     picked = jnp.dot(
         pick_ref[...], pair_ref[...].astype(jnp.bfloat16), preferred_element_type=jnp.float32
     ).astype(jnp.bfloat16)
     chosen = jnp.dot(picked, choice_ref[...], preferred_element_type=jnp.float32)
-    height = ROUNDS
+    height = ROUNDS // 2 * ENT
     first = lax.broadcasted_iota(jnp.int32, (height, 2 * SHARE), 1) < SHARE
     for b in range(NBLK):
         for d in range(0, N_DAY, 2):
@@ -161,15 +170,15 @@
 
 
 def lag_kernel(slot_ref, r_ref, lag_ref, out_ref, wide_ref):
-    height = ROUNDS
     half = ROUNDS // 2
+    height = half * ENT
     wide_ref[...] = r_ref[...].astype(jnp.float32).reshape(GROUP * height, 2 * SHARE)
     lag = lag_ref[...]
     for s in range(half):
-        real = wide_ref[pl.ds(2 * s, GROUP, stride=height), :].astype(jnp.bfloat16)
-        imag = wide_ref[pl.ds(2 * s + 1, GROUP, stride=height), :].astype(jnp.bfloat16)
-        lagged = jnp.dot(lag[:, :NB], real, preferred_element_type=jnp.float32)
-        lagged = lagged + jnp.dot(lag[:, NB:], imag, preferred_element_type=jnp.float32)
+        entries = jnp.concatenate(
+            [wide_ref[pl.ds(s * ENT + c, GROUP, stride=height), :] for c in range(ENT)], axis=0
+        ).astype(jnp.bfloat16)
+        lagged = jnp.dot(lag, entries, preferred_element_type=jnp.float32)
         lagged = lagged * (1.0 / math.sqrt(NB * DD * N_DAY))
         out_ref[slot_ref[s]] = lagged[:LAGS, :SHARE]
         out_ref[slot_ref[half + s]] = lagged[:LAGS, SHARE:]
@@ -200,7 +209,7 @@
     )(records, jnp.asarray(band_table()), jnp.asarray(day_major()))
 
     by_bin = lax.all_to_all(
-        spectra.reshape(GROUP, 2, SB * DD), group_axes, 0, 0, tiled=True
+        spectra.reshape(GROUP, ENT, SB * DD), group_axes, 0, 0, tiled=True
     ).reshape(2 * NB, SB * DD)
 
     own = pl.pallas_call(
@@ -213,11 +222,8 @@
         name="gather_days",
     )(by_bin)
 
-    groups = lax.axis_size("zq")
-    pairs = [(source, (source + 1) % groups) for source in range(groups)]
-    met = [own]
-    for _ in range(BACK):
-        met.append(lax.ppermute(met[-1], "zq", pairs))
+    everyone = lax.all_gather(own, "zq", axis=0)
+    place = lax.axis_index("zq").astype(jnp.int32).reshape(1)
 
     choice = (
         lax.broadcasted_iota(jnp.int32, (PAIRS, PAIRS), 0) == pair_order[None, :]
@@ -225,16 +231,17 @@
 
     chosen = pl.pallas_call(
         cross_kernel,
-        in_specs=vmem_specs(BACK + 4),
+        in_specs=[pl.BlockSpec(memory_space=pltpu.SMEM)] + vmem_specs(5),
         out_specs=pl.BlockSpec(memory_space=pltpu.VMEM),
-        out_shape=jax.ShapeDtypeStruct((GROUP, ROUNDS, 2 * SHARE), jnp.bfloat16),
+        out_shape=jax.ShapeDtypeStruct((GROUP, ROUNDS // 2 * ENT, 2 * SHARE), jnp.bfloat16),
         scratch_shapes=[
-            pltpu.VMEM((2 * NBLK * SB, SEEN * SB), jnp.float32),
-            pltpu.VMEM((2 * NBLK * SEEN, PAIRS), jnp.float32),
+            pltpu.VMEM((SEEN * SB, KDIM), jnp.bfloat16),
+            pltpu.VMEM((MIX * SB, SEEN * SB), jnp.float32),
+            pltpu.VMEM((MIX * SEEN, PAIRS), jnp.float32),
         ],
         compiler_params=params(),
         name="cross",
-    )(*met, jnp.asarray(spread_rows()), jnp.asarray(pick_rows()), choice)
+    )(place, own, everyone, jnp.asarray(spread_rows()), jnp.asarray(pick_rows()), choice)
 
     by_pair = lax.all_to_all(chosen, group_axes, 0, 0, tiled=True)
 
@@ -248,7 +255,7 @@
         in_specs=[pl.BlockSpec(memory_space=pltpu.SMEM)] + vmem_specs(2),
         out_specs=pl.BlockSpec(memory_space=pltpu.VMEM),
         out_shape=jax.ShapeDtypeStruct((ROUNDS, LAGS, SHARE), jnp.float32),
-        scratch_shapes=[pltpu.VMEM((GROUP * ROUNDS, 2 * SHARE), jnp.float32)],
+        scratch_shapes=[pltpu.VMEM((GROUP * ROUNDS // 2 * ENT, 2 * SHARE), jnp.float32)],
         compiler_params=params(),
         name="lags",
     )(slots, by_pair, jnp.asarray(lag_table()))

time: 102 us -> 141 us (1.38)
  waiting for transfers between devices: 27.4 us -> 74.1 us
  starting transfers between devices: 33.5 us -> 16.6 us
  between operations: 0.12 us -> 13.5 us
  blocking collectives: 24.7 us -> 17.3 us
  Pallas kernels: 8.95 us -> 10.9 us
  local copies, waits for them, and re-layouts: 5.73 us -> 7.2 us
    all_gather x0 -> x1, waiting for transfers between devices: none -> 62.6 us  [shards(): everyone = lax.all_gather(own, 'zq', axis=0)]
    ppermute x2 -> x0, starting transfers between devices: 20.3 us -> none  [shards(): met.append(lax.ppermute(met[-1], 'zq', pairs))]
    ppermute x2 -> x0, waiting for transfers between devices: 9.25 us -> none  [shards(): met.append(lax.ppermute(met[-1], 'zq', pairs))]
    all_to_all x1, blocking collectives: 24.7 us -> 17.3 us  [shards(): lax.all_to_all(spectra.reshape(GROUP, ENT, SB * DD), group_axes, 0, 0, ti...]
    all_to_all x1, waiting for transfers between devices: 18.2 us -> 11.5 us  [shards(): by_pair = lax.all_to_all(chosen, group_axes, 0, 0, tiled=True)]
    all_to_all x1, starting transfers between devices: 13.2 us -> 16.6 us  [shards(): by_pair = lax.all_to_all(chosen, group_axes, 0, 0, tiled=True)]
    unnamed x16 -> x18, local copies, waits for them, and re-layouts: 4.53 us -> 6.11 us
  transfers between devices with their start and end apart: 3 -> 2, of which waited for: 3 -> 2; matrix products, arithmetic and copies ran while one was open for 1% -> 1% of each run, Pallas kernels for 0% -> 0%
where the time goes in v2:
time: 141 us
  waiting for transfers between devices  74.1 us (53%)
  blocking collectives  17.3 us (12%)
  starting transfers between devices  16.6 us (12%)
  between operations  13.5 us (10%)
  Pallas kernels  10.9 us (8%)
  local copies, waits for them, and re-layouts  7.2 us (5%)
    all_gather x1, waiting for transfers between devices, shards(): everyone = lax.all_gather(own, 'zq', axis=0)  62.6 us
    all_to_all x1, blocking collectives, shards(): lax.all_to_all(spectra.reshape(GROUP, ENT, SB * DD), group_axes, 0, 0, ti...  17.3 us
    all_to_all x1, starting transfers between devices, shards(): by_pair = lax.all_to_all(chosen, group_axes, 0, 0, tiled=True)  16.6 us
    all_to_all x1, waiting for transfers between devices, shards(): by_pair = lax.all_to_all(chosen, group_axes, 0, 0, tiled=True)  11.5 us
    unnamed x18, local copies, waits for them, and re-layouts  6.11 us
    pallas_call x1, Pallas kernels, shards(): pl.pallas_call(cross_kernel, in_specs=[pl.BlockSpec(memory_space=pltpu.SM...  4.79 us
    pallas_call x1, Pallas kernels, shards(): pl.pallas_call(spectra_kernel, grid=(2,), in_specs=[pl.BlockSpec((HALF, D...  3.95 us
  transfers between devices with their start and end apart: 2, of which 2 were waited for; matrix products, arithmetic and copies ran while one was open for 1% of the time, Pallas kernels for 0%

profile of v2, /device:TPU:1, one launch (start us, length us, event | category | flops | bytes accessed | tf_op | source)
XLA Modules:
  0.0 140.5 jit_solution(1404200538578284981)
XLA Ops:
  6.5 0.0 all-gather.3.cloned.1.call-start
  6.5 0.0 copy-start
  6.5 1.9 %copy-done = bf16[32,8,6000]{2,1,0:T(8,128)(2,1)S(1)} copy-done((bf16[32,8,6000]{2,1,0:T(8,128)(2,1)S(1)}, bf16[32,8,6000]{2,1,0:T(8,128)(2,1)}, u32[]{:S(2)}) %copy-start) | copy-done | bytes 3072024
  8.4 0.0 copy-start.1
  8.4 1.9 %copy-done.1 = bf16[256,6000]{1,0:T(8,128)(2,1)S(1)} copy-done((bf16[256,6000]{1,0:T(8,128)(2,1)S(1)}, bf16[256,6000]{1,0:T(8,128)(2,1)}, u32[]{:S(2)}) %copy-start.1) | copy-done | bytes 3072024
  10.3 0.0 copy-start.6
  10.3 0.8 copy-done.6
  11.0 0.0 copy-start.7
  11.0 0.0 copy-start.3
  11.0 0.0 copy-start.4
  11.0 3.9 %spectra.1 = bf16[256,256]{1,0:T(8,128)(2,1)S(1)} custom-call(bf16[32,8,6000]{2,1,0:T(8,128)(2,1)S(1)} %copy-done, bf16[256,6000]{1,0:T(8,128)(2,1)S(1)} %copy-done.1, bf16[128,128]{1,0:T(8,128)(2,1)S(1)} %copy-done.6), custom_call_target="tpu_custom_call" | custom-call | tf_op jit(solution)/shard_map/spectra/pallas_call | solution.py:197
  15.0 17.3 %all_to_all.10 = bf16[32,8,256]{2,1,0:T(8,128)(2,1)S(1)} all-to-all(bf16[32,8,256]{2,1,0:T(8,128)(2,1)S(1)} %bitcast.5), channel_id=1, replica_groups=mesh['zq'=16,'zr'=1,'xh'=2,'day'=16] {'zr','xh','day'}, dimensions={0} | all-to-all | bytes 262144 | tf_op jit(solution)/shard_map/all_to_all | solution.py:211
  32.3 0.8 gather_days.1.own_ref
  33.1 0.0 all-gather.3.cloned.1.call-update
  33.1 0.0 copy-done.7
  33.1 0.9 fusion.choice_ref
  34.0 62.6 %all-gather.3.cloned.1.call-done = bf16[1024,1024]{1,0:T(8,128)(2,1)} async-done(((bf16[64,1024]{1,0:T(8,128)(2,1)}), bf16[1024,1024]{1,0:T(8,128)(2,1)}) %all-gather.3.cloned.1.call-update) | async-done | bytes 2097168 | tf_op jit(solution)/shard_map/all_gather | solution.py:225
  96.6 0.0 copy-done.3
  96.6 0.0 copy-done.4
  96.6 0.0 copy-start.2
  96.6 1.6 %copy-done.2 = bf16[1024,1024]{1,0:T(8,128)(2,1)S(1)} copy-done((bf16[1024,1024]{1,0:T(8,128)(2,1)S(1)}, bf16[1024,1024]{1,0:T(8,128)(2,1)}, u32[]{:S(2)}) %copy-start.2) | copy-done | bytes 2097176
  98.2 0.0 copy-start.8
  98.2 0.0 copy-start.5
  98.2 4.8 %cross.1 = bf16[32,64,128]{2,1,0:T(8,128)(2,1)} custom-call(s32[1]{0:T(128)} %bitcast.place_ref, bf16[64,1024]{1,0:T(8,128)(2,1)} %gather_days.1.own_ref, bf16[16,64,1024]{2,1,0:T(8,128)(2,1)S(1)} %bitcast.4, bf16[512,64]{1,0:T(8,128)(2,1)S(1)} %copy-done.4, bf16[256,288]{1,0:T(8,128)(2,1)S(1)} %copy-done.3, bf16[1024,1024]{1,0:T(8,128)(2,1)S(1)} %fusion.choice_ref), custom_call_target="tpu_custom_call" | custom-call | tf_op jit(solution)/shard_map/cross/pallas_call | solution.py:232
  103.0 16.6 %all-to-all-start.1 = ((bf16[32,64,128]{2,1,0:T(8,128)(2,1)}), bf16[32,64,128]{2,1,0:T(8,128)(2,1)S(1)}, u32[]{:S(2)}, u32[]{:S(2)}) async-start(bf16[32,64,128]{2,1,0:T(8,128)(2,1)} %cross.1), calls=%async_computation.1 | async-start | bytes 1048576 | tf_op jit(solution)/shard_map/all_to_all | solution.py:246
  119.5 0.0 copy-done.8
  119.5 0.1 select_reduce_fusion.slot_ref
  119.7 11.5 %all-to-all-done.1.r_ref = bf16[32,64,128]{2,1,0:T(8,128)(2,1)S(1)} async-done(((bf16[32,64,128]{2,1,0:T(8,128)(2,1)}), bf16[32,64,128]{2,1,0:T(8,128)(2,1)S(1)}, u32[]{:S(2)}, u32[]{:S(2)}) %all-to-all-start.1) | async-done | bytes 524320 | tf_op jit(solution)/shard_map/all_to_all | solution.py:246
  131.2 0.0 copy-done.5
  131.2 1.4 %lags.1 = f32[16,101,64]{2,1,0:T(8,128)S(1)} custom-call(s32[16]{0:T(128)S(1)} %select_reduce_fusion.slot_ref, bf16[32,64,128]{2,1,0:T(8,128)(2,1)S(1)} %all-to-all-done.1.r_ref, bf16[104,256]{1,0:T(8,128)(2,1)S(1)} %copy-done.5), custom_call_target="tpu_custom_call" | custom-call | tf_op jit(solution)/shard_map/lags/pallas_call | solution.py:253
  132.6 1.1 copy.10
Async XLA Ops:
  6.5 90.0 %all-gather.3.cloned.1.call-start = ((), (), s32[]{:S(2)}) async-start(), calls=%async_computation.2 | async-start | bytes 2228224 | tf_op jit(solution)/shard_map/all_gather | solution.py:225
  6.5 1.9 %copy-start = (bf16[32,8,6000]{2,1,0:T(8,128)(2,1)S(1)}, bf16[32,8,6000]{2,1,0:T(8,128)(2,1)}, u32[]{:S(2)}) copy-start(bf16[32,8,6000]{2,1,0:T(8,128)(2,1)} %x_ref.1) | copy-start | bytes 9216004
  8.4 1.9 %copy-start.1 = (bf16[256,6000]{1,0:T(8,128)(2,1)S(1)}, bf16[256,6000]{1,0:T(8,128)(2,1)}, u32[]{:S(2)}) copy-start(bf16[256,6000]{1,0:T(8,128)(2,1)} %constant.18.clone.band_ref) | copy-start | bytes 9216004
  10.3 0.8 copy-start.6
  11.0 22.1 %copy-start.7 = (s32[1024]{0:T(1024)S(1)}, s32[1024]{0:T(1024)}, u32[]{:S(2)}) copy-start(s32[1024]{0:T(1024)} %param.10) | copy-start | bytes 12292
  11.0 85.5 %copy-start.3 = (bf16[256,288]{1,0:T(8,128)(2,1)S(1)}, bf16[256,288]{1,0:T(8,128)(2,1)}, u32[]{:S(2)}) copy-start(bf16[256,288]{1,0:T(8,128)(2,1)} %constant.21.clone.pick_ref) | copy-start | bytes 442372
  11.0 85.5 %copy-start.4 = (bf16[512,64]{1,0:T(8,128)(2,1)S(1)}, bf16[512,64]{1,0:T(8,128)(2,1)}, u32[]{:S(2)}) copy-start(bf16[512,64]{1,0:T(8,128)(2,1)} %constant.20.clone.spread_ref) | copy-start | bytes 196612
  96.6 1.6 %copy-start.2 = (bf16[1024,1024]{1,0:T(8,128)(2,1)S(1)}, bf16[1024,1024]{1,0:T(8,128)(2,1)}, u32[]{:S(2)}) copy-start(bf16[1024,1024]{1,0:T(8,128)(2,1)} %all-gather.3.cloned.1.call-done) | copy-start | bytes 6291460
  98.2 21.4 %copy-start.8 = (s32[16]{0:T(128)S(1)}, s32[16]{0:T(128)}, u32[]{:S(2)}) copy-start(s32[16]{0:T(128)} %param.9) | copy-start | bytes 196
  98.2 33.0 %copy-start.5 = (bf16[104,256]{1,0:T(8,128)(2,1)S(1)}, bf16[104,256]{1,0:T(8,128)(2,1)}, u32[]{:S(2)}) copy-start(bf16[104,256]{1,0:T(8,128)(2,1)} %constant.22.clone.lag_ref) | copy-start | bytes 159748
  103.0 28.2 %all-to-all-start.1 = ((bf16[32,64,128]{2,1,0:T(8,128)(2,1)}), bf16[32,64,128]{2,1,0:T(8,128)(2,1)S(1)}, u32[]{:S(2)}, u32[]{:S(2)}) async-start(bf16[32,64,128]{2,1,0:T(8,128)(2,1)} %cross.1), calls=%async_computation.1 | async-start | bytes 1048576 | tf_op jit(solution)/shard_map/all_to_all | solution.py:246
Sparse Core Ops, SparseCore 0:
  33.2 63.2 all-gather.2

commit v3 on v2

--- a/solution.py
+++ b/solution.py
@@ -21,7 +21,7 @@
 N_DAY = 16
 N_HI = 2
 PLANES = 16
-ZG = 1
+ZG = 2
 NBLK = ZG * N_HI
 GROUP = NBLK * N_DAY
 KB = NB // GROUP
@@ -36,6 +36,7 @@
 SHARE = PAIRS // N_DAY
 LAG_ROWS = 104
 HALF = SB // 2
+STREAMS = 2
 VMEM = 44 * 1024 * 1024
 
 assert NB == GROUP * KB and ROUNDS == BACK * NBLK
@@ -107,7 +108,8 @@
     ).astype(jnp.bfloat16)
 
 
-def gather_days_kernel(r_ref, out_ref, wide_ref):
+def gather_days_kernel(r_ref, *refs):
+    out_refs, wide_ref = refs[:-1], refs[-1]
     turned = r_ref[...].astype(jnp.float32).T
     for half in range(2):
         for e in range(DD):
@@ -117,13 +119,22 @@
                          e * WIDTH : (e + 1) * WIDTH] = (
                     turned[row : row + HALF, b * WIDTH : (b + 1) * WIDTH]
                 )
-    out_ref[...] = wide_ref[...].astype(jnp.bfloat16)
-
-
-def cross_kernel(
-    place_ref, own_ref, all_ref, spread_ref, pick_ref, choice_ref, out_ref, met_ref, cross_ref, pair_ref
-):
-    own = own_ref[...]
+    share = NBLK * SB // STREAMS
+    for part, out_ref in enumerate(out_refs):
+        out_ref[...] = wide_ref[part * share : (part + 1) * share, :].astype(jnp.bfloat16)
+
+
+def cross_kernel(*refs):
+    piece_refs = refs[: (BACK + 1) * STREAMS]
+    spread_ref, pick_ref, choice_ref, out_ref, met_ref, cross_ref, pair_ref = refs[
+        (BACK + 1) * STREAMS :
+    ]
+    share = NBLK * SB // STREAMS
+    for step in range(BACK + 1):
+        for part in range(STREAMS):
+            start = (BACK - step) * NBLK * SB + part * share
+            met_ref[start : start + share, :] = piece_refs[step * STREAMS + part][...]
+    own = met_ref[BACK * NBLK * SB :, :]
     wide = own.astype(jnp.float32)
     lane = lax.broadcasted_iota(jnp.int32, wide.shape, 1)
     turned = jnp.where(
@@ -138,10 +149,6 @@
         jnp.dot(spread, turned, preferred_element_type=jnp.float32),
     )
     left = jnp.where(row // NBLK % KB == lane % KB, left, 0.0).astype(jnp.bfloat16)
-    height = NBLK * SB
-    for step in range(BACK + 1):
-        source = lax.rem(place_ref[0] + (GROUPS - BACK + step), GROUPS)
-        met_ref[step * height : (step + 1) * height, :] = all_ref[source]
     cross_ref[...] = lax.dot_general(
         left, met_ref[...], (((1,), (1,)), ((), ())), preferred_element_type=jnp.float32
     )
@@ -178,10 +185,12 @@
         entries = jnp.concatenate(
             [wide_ref[pl.ds(s * ENT + c, GROUP, stride=height), :] for c in range(ENT)], axis=0
         ).astype(jnp.bfloat16)
-        lagged = jnp.dot(lag, entries, preferred_element_type=jnp.float32)
+        lagged = lax.dot_general(
+            entries, lag, (((0,), (1,)), ((), ())), preferred_element_type=jnp.float32
+        )
         lagged = lagged * (1.0 / math.sqrt(NB * DD * N_DAY))
-        out_ref[slot_ref[s]] = lagged[:LAGS, :SHARE]
-        out_ref[slot_ref[half + s]] = lagged[:LAGS, SHARE:]
+        out_ref[slot_ref[s]] = lagged[:SHARE, :LAGS]
+        out_ref[slot_ref[half + s]] = lagged[SHARE:, :LAGS]
 
 
 def params():
@@ -215,15 +224,17 @@
     own = pl.pallas_call(
         gather_days_kernel,
         in_specs=vmem_specs(1),
-        out_specs=pl.BlockSpec(memory_space=pltpu.VMEM),
-        out_shape=jax.ShapeDtypeStruct((NBLK * SB, KDIM), jnp.bfloat16),
+        out_specs=vmem_specs(STREAMS),
+        out_shape=[jax.ShapeDtypeStruct((NBLK * SB // STREAMS, KDIM), jnp.bfloat16)] * STREAMS,
         scratch_shapes=[pltpu.VMEM((NBLK * SB, KDIM), jnp.float32)],
         compiler_params=params(),
         name="gather_days",
     )(by_bin)
 
-    everyone = lax.all_gather(own, "zq", axis=0)
-    place = lax.axis_index("zq").astype(jnp.int32).reshape(1)
+    pairs = [(source, (source + 1) % GROUPS) for source in range(GROUPS)]
+    pieces = list(own)
+    for step in range(BACK):
+        pieces += [lax.ppermute(piece, "zq", pairs) for piece in pieces[step * STREAMS :]]
 
     choice = (
         lax.broadcasted_iota(jnp.int32, (PAIRS, PAIRS), 0) == pair_order[None, :]
@@ -231,7 +242,7 @@
 
     chosen = pl.pallas_call(
         cross_kernel,
-        in_specs=[pl.BlockSpec(memory_space=pltpu.SMEM)] + vmem_specs(5),
+        in_specs=vmem_specs((BACK + 1) * STREAMS + 3),
         out_specs=pl.BlockSpec(memory_space=pltpu.VMEM),
         out_shape=jax.ShapeDtypeStruct((GROUP, ROUNDS // 2 * ENT, 2 * SHARE), jnp.bfloat16),
         scratch_shapes=[
@@ -241,7 +252,7 @@
         ],
         compiler_params=params(),
         name="cross",
-    )(place, own, everyone, jnp.asarray(spread_rows()), jnp.asarray(pick_rows()), choice)
+    )(*pieces, jnp.asarray(spread_rows()), jnp.asarray(pick_rows()), choice)
 
     by_pair = lax.all_to_all(chosen, group_axes, 0, 0, tiled=True)
 
@@ -250,15 +261,16 @@
         jnp.where(offsets[None, :] == steps[:, None], steps[None, :], 0), axis=1
     ).astype(jnp.int32)
 
-    return pl.pallas_call(
+    lagged = pl.pallas_call(
         lag_kernel,
         in_specs=[pl.BlockSpec(memory_space=pltpu.SMEM)] + vmem_specs(2),
         out_specs=pl.BlockSpec(memory_space=pltpu.VMEM),
-        out_shape=jax.ShapeDtypeStruct((ROUNDS, LAGS, SHARE), jnp.float32),
+        out_shape=jax.ShapeDtypeStruct((ROUNDS, SHARE, LAGS), jnp.float32),
         scratch_shapes=[pltpu.VMEM((GROUP * ROUNDS // 2 * ENT, 2 * SHARE), jnp.float32)],
         compiler_params=params(),
         name="lags",
     )(slots, by_pair, jnp.asarray(lag_table()))
+    return jnp.transpose(lagged, (0, 2, 1))
 
 
 def solution(mesh):

time: 141 us -> 95.8 us (0.68)
  waiting for transfers between devices: 74.1 us -> 15.6 us
  starting transfers between devices: 16.6 us -> 45.2 us
  between operations: 13.5 us -> 0.2 us
  local copies, waits for them, and re-layouts: 7.2 us -> 4.6 us
  blocking collectives: 17.3 us -> 18.9 us
    all_gather x1 -> x0, waiting for transfers between devices: 62.6 us -> none  [shards(): everyone = lax.all_gather(own, 'zq', axis=0)]
    ppermute x0 -> x8, starting transfers between devices: none -> 35.6 us  [shards(): lax.ppermute(piece, 'zq', pairs)]
    all_to_all x1, starting transfers between devices: 16.6 us -> 9.6 us  [shards(): by_pair = lax.all_to_all(chosen, group_axes, 0, 0, tiled=True)]
    ppermute x0 -> x8, waiting for transfers between devices: none -> 3.59 us  [shards(): lax.ppermute(piece, 'zq', pairs)]
    pallas_call x2, Pallas kernels: 5.55 us -> 3.6 us  [the longest x1 3.39 us: shards(): pl.pallas_call(cross_kernel, in_specs=vmem_specs((BACK + 1) * STREAMS + 3...]
    unnamed x18 -> x16, local copies, waits for them, and re-layouts: 6.11 us -> 4.53 us
    all_to_all x1, blocking collectives: 17.3 us -> 18.9 us  [shards(): lax.all_to_all(spectra.reshape(GROUP, ENT, SB * DD), group_axes, 0, 0, ti...]
  transfers between devices with their start and end apart: 2 -> 9, of which waited for: 2 -> 3; matrix products, arithmetic and copies ran while one was open for 1% -> 1% of each run, Pallas kernels for 0% -> 0%
where the time goes in v3:
time: 95.8 us; the launch traced here: 95.2 us
  starting transfers between devices  45.2 us (47%)
  blocking collectives  18.9 us (20%)
  waiting for transfers between devices  15.6 us (16%)
  Pallas kernels  9.71 us (10%)
  local copies, waits for them, and re-layouts  4.6 us (5%)
  other arithmetic  1 us (1%)
    ppermute x8, starting transfers between devices, shards(): lax.ppermute(piece, 'zq', pairs)  35.6 us
    all_to_all x1, blocking collectives, shards(): lax.all_to_all(spectra.reshape(GROUP, ENT, SB * DD), group_axes, 0, 0, ti...  18.9 us
    all_to_all x1, waiting for transfers between devices, shards(): by_pair = lax.all_to_all(chosen, group_axes, 0, 0, tiled=True)  12.1 us
    all_to_all x1, starting transfers between devices, shards(): by_pair = lax.all_to_all(chosen, group_axes, 0, 0, tiled=True)  9.6 us
    unnamed x16, local copies, waits for them, and re-layouts  4.53 us
    pallas_call x1, Pallas kernels, shards(): pl.pallas_call(spectra_kernel, grid=(2,), in_specs=[pl.BlockSpec((HALF, D...  3.95 us
    ppermute x8, waiting for transfers between devices, shards(): lax.ppermute(piece, 'zq', pairs)  3.59 us
    pallas_call x1, Pallas kernels, shards(): pl.pallas_call(cross_kernel, in_specs=vmem_specs((BACK + 1) * STREAMS + 3...  3.39 us
  transfers between devices with their start and end apart: 9, of which 3 were waited for; matrix products, arithmetic and copies ran while one was open for 1% of the time, Pallas kernels for 0%

profile of v3, /device:TPU:1, one launch (start us, length us, event | category | flops | bytes accessed | tf_op | source)
XLA Modules:
  0.0 95.2 jit_solution(6219639568863741568)
XLA Ops:
  0.0 0.0 copy-start
  0.0 1.9 %copy-done = bf16[32,8,6000]{2,1,0:T(8,128)(2,1)S(1)} copy-done((bf16[32,8,6000]{2,1,0:T(8,128)(2,1)S(1)}, bf16[32,8,6000]{2,1,0:T(8,128)(2,1)}, u32[]{:S(2)}) %copy-start) | copy-done | bytes 3072024
  1.9 0.0 copy-start.1
  1.9 1.9 %copy-done.1 = bf16[256,6000]{1,0:T(8,128)(2,1)S(1)} copy-done((bf16[256,6000]{1,0:T(8,128)(2,1)S(1)}, bf16[256,6000]{1,0:T(8,128)(2,1)}, u32[]{:S(2)}) %copy-start.1) | copy-done | bytes 3072024
  3.7 0.0 copy-start.5
  3.7 0.8 copy-done.5
  4.5 0.0 copy-start.6
  4.5 3.9 %spectra.1 = bf16[256,256]{1,0:T(8,128)(2,1)S(1)} custom-call(bf16[32,8,6000]{2,1,0:T(8,128)(2,1)S(1)} %copy-done, bf16[256,6000]{1,0:T(8,128)(2,1)S(1)} %copy-done.1, bf16[128,128]{1,0:T(8,128)(2,1)S(1)} %copy-done.5), custom_call_target="tpu_custom_call" | custom-call | tf_op jit(solution)/shard_map/spectra/pallas_call | solution.py:206
  8.5 0.0 copy-start.2
  8.5 0.0 copy-start.3
  8.5 18.9 %all_to_all.10 = bf16[64,4,256]{2,1,0:T(4,128)(2,1)S(1)} all-to-all(bf16[64,4,256]{2,1,0:T(4,128)(2,1)S(1)} %reshape.8), channel_id=1, replica_groups=mesh['zq'=8,'zr'=2,'xh'=2,'day'=16] {'zr','xh','day'}, dimensions={0} | all-to-all | bytes 262144 | tf_op jit(solution)/shard_map/all_to_all | solution.py:220
  27.4 0.2 gather_days.1
  27.6 4.8 %collective-permute-start = (bf16[64,512]{1,0:T(8,128)(2,1)S(1)}, bf16[64,512]{1,0:T(8,128)(2,1)S(1)}, u32[]{:S(2)}, u32[]{:S(2)}) collective-permute-start(bf16[64,512]{1,0:T(8,128)(2,1)S(1)} %get-tuple-element.7.refs_0_), channel_id=1, source_target_pairs={{0,64},{64,128},{128,192},{192,256},{256,320},{320,384},{384,448},... | collective-permute-start | bytes 196616 | tf_op jit(solution)/shard_map/ppermute | solution.py:237
  32.5 0.0 copy-start.7
  32.5 0.0 copy-start.4
  32.5 6.2 %collective-permute-start.1 = (bf16[64,512]{1,0:T(8,128)(2,1)S(1)}, bf16[64,512]{1,0:T(8,128)(2,1)S(1)}, u32[]{:S(2)}, u32[]{:S(2)}) collective-permute-start(bf16[64,512]{1,0:T(8,128)(2,1)S(1)} %get-tuple-element.8.refs_1_), channel_id=1, source_target_pairs={{0,64},{64,128},{128,192},{192,256},{256,320},{320,384},{384,448},... | collective-permute-start | bytes 196616 | tf_op jit(solution)/shard_map/ppermute | solution.py:237
  38.7 1.6 %collective-permute-done.refs_2_ = bf16[64,512]{1,0:T(8,128)(2,1)S(1)} collective-permute-done((bf16[64,512]{1,0:T(8,128)(2,1)S(1)}, bf16[64,512]{1,0:T(8,128)(2,1)S(1)}, u32[]{:S(2)}, u32[]{:S(2)}) %collective-permute-start) | collective-permute-done | bytes 65568 | tf_op jit(solution)/shard_map/ppermute | solution.py:237
  40.4 3.3 %collective-permute-start.2 = (bf16[64,512]{1,0:T(8,128)(2,1)S(1)}, bf16[64,512]{1,0:T(8,128)(2,1)S(1)}, u32[]{:S(2)}, u32[]{:S(2)}) collective-permute-start(bf16[64,512]{1,0:T(8,128)(2,1)S(1)} %collective-permute-done.refs_2_), channel_id=1, source_target_pairs={{0,64},{64,128},{128,192},{192,256},{256,320},{320,384},{384,448},... | collective-permute-start | bytes 196616 | tf_op jit(solution)/shard_map/ppermute | solution.py:237
  43.7 0.0 collective-permute-done.1.refs_3_
  43.7 5.2 %collective-permute-start.3 = (bf16[64,512]{1,0:T(8,128)(2,1)S(1)}, bf16[64,512]{1,0:T(8,128)(2,1)S(1)}, u32[]{:S(2)}, u32[]{:S(2)}) collective-permute-start(bf16[64,512]{1,0:T(8,128)(2,1)S(1)} %collective-permute-done.1.refs_3_), channel_id=1, source_target_pairs={{0,64},{64,128},{128,192},{192,256},{256,320},{320,384},{384,448},... | collective-permute-start | bytes 196616 | tf_op jit(solution)/shard_map/ppermute | solution.py:237
  48.9 0.0 collective-permute-done.2.refs_4_
  48.9 3.1 %collective-permute-start.4 = (bf16[64,512]{1,0:T(8,128)(2,1)S(1)}, bf16[64,512]{1,0:T(8,128)(2,1)S(1)}, u32[]{:S(2)}, u32[]{:S(2)}) collective-permute-start(bf16[64,512]{1,0:T(8,128)(2,1)S(1)} %collective-permute-done.2.refs_4_), channel_id=1, source_target_pairs={{0,64},{64,128},{128,192},{192,256},{256,320},{320,384},{384,448},... | collective-permute-start | bytes 196616 | tf_op jit(solution)/shard_map/ppermute | solution.py:237
  52.0 0.0 collective-permute-done.3.refs_5_
  52.0 4.9 %collective-permute-start.5 = (bf16[64,512]{1,0:T(8,128)(2,1)S(1)}, bf16[64,512]{1,0:T(8,128)(2,1)S(1)}, u32[]{:S(2)}, u32[]{:S(2)}) collective-permute-start(bf16[64,512]{1,0:T(8,128)(2,1)S(1)} %collective-permute-done.3.refs_5_), channel_id=1, source_target_pairs={{0,64},{64,128},{128,192},{192,256},{256,320},{320,384},{384,448},... | collective-permute-start | bytes 196616 | tf_op jit(solution)/shard_map/ppermute | solution.py:237
  57.0 0.0 collective-permute-done.4.refs_6_
  57.0 3.3 %collective-permute-start.6 = (bf16[64,512]{1,0:T(8,128)(2,1)S(1)}, bf16[64,512]{1,0:T(8,128)(2,1)S(1)}, u32[]{:S(2)}, u32[]{:S(2)}) collective-permute-start(bf16[64,512]{1,0:T(8,128)(2,1)S(1)} %collective-permute-done.4.refs_6_), channel_id=1, source_target_pairs={{0,64},{64,128},{128,192},{192,256},{256,320},{320,384},{384,448},... | collective-permute-start | bytes 196616 | tf_op jit(solution)/shard_map/ppermute | solution.py:237
  60.3 0.0 collective-permute-done.5.refs_7_
  60.3 4.7 %collective-permute-start.7 = (bf16[64,512]{1,0:T(8,128)(2,1)S(1)}, bf16[64,512]{1,0:T(8,128)(2,1)S(1)}, u32[]{:S(2)}, u32[]{:S(2)}) collective-permute-start(bf16[64,512]{1,0:T(8,128)(2,1)S(1)} %collective-permute-done.5.refs_7_), channel_id=1, source_target_pairs={{0,64},{64,128},{128,192},{192,256},{256,320},{320,384},{384,448},... | collective-permute-start | bytes 196616 | tf_op jit(solution)/shard_map/ppermute | solution.py:237
  65.0 0.0 copy-done.6
  65.0 0.9 fusion.refs_12_
  65.9 0.0 collective-permute-done.6.refs_8_
  65.9 2.0 %collective-permute-done.7.refs_9_ = bf16[64,512]{1,0:T(8,128)(2,1)S(1)} collective-permute-done((bf16[64,512]{1,0:T(8,128)(2,1)S(1)}, bf16[64,512]{1,0:T(8,128)(2,1)S(1)}, u32[]{:S(2)}, u32[]{:S(2)}) %collective-permute-start.7) | collective-permute-done | bytes 65568 | tf_op jit(solution)/shard_map/ppermute | solution.py:237
  67.9 0.0 copy-done.2
  67.9 0.0 copy-done.3
  67.9 3.4 %cross.1 = bf16[64,32,128]{2,1,0:T(8,128)(2,1)} custom-call(bf16[64,512]{1,0:T(8,128)(2,1)S(1)} %get-tuple-element.7.refs_0_, bf16[64,512]{1,0:T(8,128)(2,1)S(1)} %get-tuple-element.8.refs_1_, bf16[64,512]{1,0:T(8,128)(2,1)S(1)} %collective-permute-done.refs_2_, bf16[64,512]{1,0:T(8,128)(2,1)S(1)} %collective-permute-done.1.refs_3_, ...), custom_call_target="tpu_custom_call" | custom-call | tf_op jit(solution)/shard_map/cross/pallas_call | solution.py:243
  71.3 9.6 %all-to-all-start.1 = ((bf16[64,32,128]{2,1,0:T(8,128)(2,1)}), bf16[64,32,128]{2,1,0:T(8,128)(2,1)S(1)}, u32[]{:S(2)}, u32[]{:S(2)}) async-start(bf16[64,32,128]{2,1,0:T(8,128)(2,1)} %cross.1), calls=%async_computation.1 | async-start | bytes 1048576 | tf_op jit(solution)/shard_map/all_to_all | solution.py:257
  80.9 0.0 copy-done.7
  80.9 0.1 select_reduce_fusion.slot_ref
  81.0 12.1 %all-to-all-done.1.r_ref = bf16[64,32,128]{2,1,0:T(8,128)(2,1)S(1)} async-done(((bf16[64,32,128]{2,1,0:T(8,128)(2,1)}), bf16[64,32,128]{2,1,0:T(8,128)(2,1)S(1)}, u32[]{:S(2)}, u32[]{:S(2)}) %all-to-all-start.1) | async-done | bytes 524320 | tf_op jit(solution)/shard_map/all_to_all | solution.py:257
  93.1 0.0 copy-done.4
  93.1 2.2 %lags.1 = f32[16,64,101]{2,1,0:T(8,128)} custom-call(s32[16]{0:T(128)S(1)} %select_reduce_fusion.slot_ref, bf16[64,32,128]{2,1,0:T(8,128)(2,1)S(1)} %all-to-all-done.1.r_ref, bf16[104,256]{1,0:T(8,128)(2,1)S(1)} %copy-done.4), custom_call_target="tpu_custom_call" | custom-call | tf_op jit(solution)/shard_map/lags/pallas_call | solution.py:264
  (2 shorter events, 0.1 us)
Async XLA Ops:
  0.0 1.9 %copy-start = (bf16[32,8,6000]{2,1,0:T(8,128)(2,1)S(1)}, bf16[32,8,6000]{2,1,0:T(8,128)(2,1)}, u32[]{:S(2)}) copy-start(bf16[32,8,6000]{2,1,0:T(8,128)(2,1)} %x_ref.1) | copy-start | bytes 9216004
  1.9 1.9 %copy-start.1 = (bf16[256,6000]{1,0:T(8,128)(2,1)S(1)}, bf16[256,6000]{1,0:T(8,128)(2,1)}, u32[]{:S(2)}) copy-start(bf16[256,6000]{1,0:T(8,128)(2,1)} %constant.12.clone.band_ref) | copy-start | bytes 9216004
  3.7 0.8 copy-start.5
  4.5 60.5 %copy-start.6 = (s32[1024]{0:T(1024)S(1)}, s32[1024]{0:T(1024)}, u32[]{:S(2)}) copy-start(s32[1024]{0:T(1024)} %param.10) | copy-start | bytes 12292
  8.5 59.4 %copy-start.2 = (bf16[256,320]{1,0:T(8,128)(2,1)S(1)}, bf16[256,320]{1,0:T(8,128)(2,1)}, u32[]{:S(2)}) copy-start(bf16[256,320]{1,0:T(8,128)(2,1)} %constant.15.clone.refs_11_) | copy-start | bytes 491524
  8.5 59.4 %copy-start.3 = (bf16[512,128]{1,0:T(8,128)(2,1)S(1)}, bf16[512,128]{1,0:T(8,128)(2,1)}, u32[]{:S(2)}) copy-start(bf16[512,128]{1,0:T(8,128)(2,1)} %constant.14.clone.refs_10_) | copy-start | bytes 393220
  27.6 12.7 %collective-permute-start = (bf16[64,512]{1,0:T(8,128)(2,1)S(1)}, bf16[64,512]{1,0:T(8,128)(2,1)S(1)}, u32[]{:S(2)}, u32[]{:S(2)}) collective-permute-start(bf16[64,512]{1,0:T(8,128)(2,1)S(1)} %get-tuple-element.7.refs_0_), channel_id=1, source_target_pairs={{0,64},{64,128},{128,192},{192,256},{256,320},{320,384},{384,448},... | collective-permute-start | bytes 196616 | tf_op jit(solution)/shard_map/ppermute | solution.py:237
  32.5 48.4 %copy-start.7 = (s32[16]{0:T(128)S(1)}, s32[16]{0:T(128)}, u32[]{:S(2)}) copy-start(s32[16]{0:T(128)} %param.9) | copy-start | bytes 196
  32.5 60.6 %copy-start.4 = (bf16[104,256]{1,0:T(8,128)(2,1)S(1)}, bf16[104,256]{1,0:T(8,128)(2,1)}, u32[]{:S(2)}) copy-start(bf16[104,256]{1,0:T(8,128)(2,1)} %constant.16.clone.lag_ref) | copy-start | bytes 159748
  32.5 11.2 %collective-permute-start.1 = (bf16[64,512]{1,0:T(8,128)(2,1)S(1)}, bf16[64,512]{1,0:T(8,128)(2,1)S(1)}, u32[]{:S(2)}, u32[]{:S(2)}) collective-permute-start(bf16[64,512]{1,0:T(8,128)(2,1)S(1)} %get-tuple-element.8.refs_1_), channel_id=1, source_target_pairs={{0,64},{64,128},{128,192},{192,256},{256,320},{320,384},{384,448},... | collective-permute-start | bytes 196616 | tf_op jit(solution)/shard_map/ppermute | solution.py:237
  40.4 8.5 %collective-permute-start.2 = (bf16[64,512]{1,0:T(8,128)(2,1)S(1)}, bf16[64,512]{1,0:T(8,128)(2,1)S(1)}, u32[]{:S(2)}, u32[]{:S(2)}) collective-permute-start(bf16[64,512]{1,0:T(8,128)(2,1)S(1)} %collective-permute-done.refs_2_), channel_id=1, source_target_pairs={{0,64},{64,128},{128,192},{192,256},{256,320},{320,384},{384,448},... | collective-permute-start | bytes 196616 | tf_op jit(solution)/shard_map/ppermute | solution.py:237
  43.7 8.3 %collective-permute-start.3 = (bf16[64,512]{1,0:T(8,128)(2,1)S(1)}, bf16[64,512]{1,0:T(8,128)(2,1)S(1)}, u32[]{:S(2)}, u32[]{:S(2)}) collective-permute-start(bf16[64,512]{1,0:T(8,128)(2,1)S(1)} %collective-permute-done.1.refs_3_), channel_id=1, source_target_pairs={{0,64},{64,128},{128,192},{192,256},{256,320},{320,384},{384,448},... | collective-permute-start | bytes 196616 | tf_op jit(solution)/shard_map/ppermute | solution.py:237
  48.9 8.1 %collective-permute-start.4 = (bf16[64,512]{1,0:T(8,128)(2,1)S(1)}, bf16[64,512]{1,0:T(8,128)(2,1)S(1)}, u32[]{:S(2)}, u32[]{:S(2)}) collective-permute-start(bf16[64,512]{1,0:T(8,128)(2,1)S(1)} %collective-permute-done.2.refs_4_), channel_id=1, source_target_pairs={{0,64},{64,128},{128,192},{192,256},{256,320},{320,384},{384,448},... | collective-permute-start | bytes 196616 | tf_op jit(solution)/shard_map/ppermute | solution.py:237
  52.0 8.3 %collective-permute-start.5 = (bf16[64,512]{1,0:T(8,128)(2,1)S(1)}, bf16[64,512]{1,0:T(8,128)(2,1)S(1)}, u32[]{:S(2)}, u32[]{:S(2)}) collective-permute-start(bf16[64,512]{1,0:T(8,128)(2,1)S(1)} %collective-permute-done.3.refs_5_), channel_id=1, source_target_pairs={{0,64},{64,128},{128,192},{192,256},{256,320},{320,384},{384,448},... | collective-permute-start | bytes 196616 | tf_op jit(solution)/shard_map/ppermute | solution.py:237
  57.0 8.9 %collective-permute-start.6 = (bf16[64,512]{1,0:T(8,128)(2,1)S(1)}, bf16[64,512]{1,0:T(8,128)(2,1)S(1)}, u32[]{:S(2)}, u32[]{:S(2)}) collective-permute-start(bf16[64,512]{1,0:T(8,128)(2,1)S(1)} %collective-permute-done.4.refs_6_), channel_id=1, source_target_pairs={{0,64},{64,128},{128,192},{192,256},{256,320},{320,384},{384,448},... | collective-permute-start | bytes 196616 | tf_op jit(solution)/shard_map/ppermute | solution.py:237
  60.3 7.6 %collective-permute-start.7 = (bf16[64,512]{1,0:T(8,128)(2,1)S(1)}, bf16[64,512]{1,0:T(8,128)(2,1)S(1)}, u32[]{:S(2)}, u32[]{:S(2)}) collective-permute-start(bf16[64,512]{1,0:T(8,128)(2,1)S(1)} %collective-permute-done.5.refs_7_), channel_id=1, source_target_pairs={{0,64},{64,128},{128,192},{192,256},{256,320},{320,384},{384,448},... | collective-permute-start | bytes 196616 | tf_op jit(solution)/shard_map/ppermute | solution.py:237
  71.3 21.8 %all-to-all-start.1 = ((bf16[64,32,128]{2,1,0:T(8,128)(2,1)}), bf16[64,32,128]{2,1,0:T(8,128)(2,1)S(1)}, u32[]{:S(2)}, u32[]{:S(2)}) async-start(bf16[64,32,128]{2,1,0:T(8,128)(2,1)} %cross.1), calls=%async_computation.1 | async-start | bytes 1048576 | tf_op jit(solution)/shard_map/all_to_all | solution.py:257

commit v4 on v2

v4 whole, which is shorter than its diff:
```python
import functools
import math

import jax
import jax.numpy as jnp
import ml_dtypes
import numpy as np
from jax import lax
from jax.experimental import pallas as pl
from jax.experimental.pallas import tpu as pltpu
from jax.sharding import Mesh
from jax.sharding import PartitionSpec as P

SB = 32
DD = 8
NT = 6000
NB = 128
K0 = 30
LAGS = 101
ROUNDS = 16
N_DAY = 16
N_HI = 2
PLANES = 16
ZG = 2
NBLK = ZG * N_HI
GROUP = NBLK * N_DAY
KB = NB // GROUP
ENT = 2 * KB
MIX = ENT * NBLK
GROUPS = PLANES // ZG
BACK = ROUNDS // NBLK
SEEN = ROUNDS + NBLK
WIDTH = N_DAY * ENT
KDIM = DD * WIDTH
PAIRS = SB * SB
SHARE = PAIRS // N_DAY
LAG_ROWS = 128
STEPS = 16 // ENT
BASE = 256
FETCHES = 8
VMEM = 44 * 1024 * 1024

assert NB == GROUP * KB and ROUNDS == BACK * NBLK


def phase_table(columns):
    bins = np.arange(NB, dtype=np.int64) + K0
    turns = (bins[:, None] * columns[None, :]) % NT
    angle = 2.0 * math.pi / NT * turns.astype(np.float64)
    return np.cos(angle).astype(ml_dtypes.bfloat16), (-np.sin(angle)).astype(ml_dtypes.bfloat16)


def band_parts():
    bins = (np.arange(NB) + K0).reshape(GROUP, 1, KB)
    bins = np.broadcast_to(bins, (GROUP, 2, KB)).reshape(2 * NB).astype(np.int64)
    imag = np.broadcast_to(np.arange(2).reshape(1, 2, 1), (GROUP, 2, KB)).reshape(2 * NB)
    unit = 2.0 * math.pi / NT
    fine = unit * (np.arange(BASE)[:, None] * bins % NT)
    coarse = unit * (np.arange(0, NT, BASE)[:, None] * bins % NT)
    with_cos = np.where(imag, -np.sin(coarse), np.cos(coarse))
    with_sin = np.where(imag, -np.cos(coarse), -np.sin(coarse))
    parts = np.concatenate([np.cos(fine), np.sin(fine), with_cos, with_sin], axis=0)
    return np.pad(parts, ((0, -len(parts) % 8), (0, 0))).astype(np.float32)


def lag_table():
    real, imag = phase_table(np.arange(LAGS, dtype=np.int64) - LAGS // 2)
    rows = np.stack([real.reshape(GROUP, KB, LAGS), imag.reshape(GROUP, KB, LAGS)], axis=1)
    rows = rows.reshape(GROUP, ENT, LAGS).transpose(2, 0, 1)
    table = np.zeros((STEPS, LAG_ROWS, GROUP, STEPS, ENT), ml_dtypes.bfloat16)
    for step in range(STEPS):
        table[step, :LAGS, :, step, :] = rows
    return table.reshape(STEPS * LAG_ROWS, GROUP * STEPS * ENT)


def spread_rows():
    table = np.zeros((MIX * SB, NBLK * SB), ml_dtypes.bfloat16)
    for i in range(SB):
        for c in range(ENT):
            for b in range(NBLK):
                table[i * MIX + c * NBLK + b, b * SB + i] = 1
    return table


def pick_rows():
    half = ROUNDS // 2
    table = np.zeros((MIX * ROUNDS, SEEN * MIX), ml_dtypes.bfloat16)
    for h in range(2):
        for b in range(NBLK):
            for s in range(half):
                for c in range(ENT):
                    met = b + ROUNDS - (h * half + s + 1)
                    row = ((h * NBLK + b) * half + s) * ENT + c
                    table[row, met * MIX + c * NBLK + b] = 1
    return table


def spectra_kernel(records_ref, parts_ref, out_ref, x_ref, angle_ref, centred_ref, sems):
    part = SB // FETCHES
    copies = [
        pltpu.make_async_copy(
            records_ref.at[pl.ds(i * part, part)], x_ref.at[pl.ds(i * part, part)], sems.at[i]
        )
        for i in range(FETCHES)
    ]
    angles = pltpu.make_async_copy(parts_ref, angle_ref, sems.at[FETCHES])
    angles.start()
    for copy in copies:
        copy.start()
    powers = []
    for i, copy in enumerate(copies):
        copy.wait()
        x = x_ref[i * part : (i + 1) * part].astype(jnp.float32).reshape(part * DD, NT)
        x = x - jnp.sum(x, axis=1, keepdims=True) * (1.0 / NT)
        powers.append(jnp.sum(x * x, axis=1, keepdims=True) * (1.0 / NT))
        centred_ref[i * part * DD : (i + 1) * part * DD, :] = x.astype(jnp.bfloat16)
    power = jnp.concatenate(powers, axis=0)
    angles.wait()
    blocks = pl.cdiv(NT, BASE)
    raw = jnp.zeros((SB * DD, 2 * NB), jnp.float32)
    for block in range(blocks):
        start, size = block * BASE, min(BASE, NT - block * BASE)
        with_cos = angle_ref[2 * BASE + block : 2 * BASE + block + 1, :]
        with_sin = angle_ref[2 * BASE + blocks + block : 2 * BASE + blocks + block + 1, :]
        table = with_cos * angle_ref[:size, :] + with_sin * angle_ref[BASE : BASE + size, :]
        raw = raw + jnp.dot(
            centred_ref[:, start : start + size], table.astype(jnp.bfloat16),
            preferred_element_type=jnp.float32,
        )
    raw = raw / jnp.sqrt(power + 1e-06)
    scale = jnp.sqrt(jnp.sum(raw * raw, axis=1, keepdims=True) * (1.0 / NB) + 1e-06)
    spectra = (raw / scale).astype(jnp.bfloat16)
    row = lax.broadcasted_iota(jnp.int32, (SB * DD, SB * DD), 0)
    column = lax.broadcasted_iota(jnp.int32, (SB * DD, SB * DD), 1)
    order = (row == column % SB * DD + column // SB).astype(jnp.float32).astype(jnp.bfloat16)
    by_entry = lax.dot_general(
        spectra, order, (((0,), (0,)), ((), ())), preferred_element_type=jnp.float32
    )
    for device in range(GROUP):
        out_ref[device] = by_entry[device * ENT : (device + 1) * ENT, :].astype(jnp.bfloat16)


def gather_days_kernel(r_ref, out_ref, wide_ref):
    turned = r_ref[...].astype(jnp.float32).T
    for e in range(DD):
        for b in range(NBLK):
            wide_ref[b * SB : (b + 1) * SB, e * WIDTH : (e + 1) * WIDTH] = (
                turned[e * SB : (e + 1) * SB, b * WIDTH : (b + 1) * WIDTH]
            )
    out_ref[...] = wide_ref[...].astype(jnp.bfloat16)


def cross_kernel(*refs):
    group_refs = refs[: BACK + 1]
    spread_ref, pick_ref, choice_ref, out_ref, met_ref, cross_ref, pair_ref = refs[BACK + 1 :]
    for step, group_ref in enumerate(group_refs):
        start = (BACK - step) * NBLK * SB
        met_ref[start : start + NBLK * SB, :] = group_ref[...]
    own = met_ref[BACK * NBLK * SB :, :]
    wide = own.astype(jnp.float32)
    lane = lax.broadcasted_iota(jnp.int32, wide.shape, 1)
    turned = jnp.where(
        lane % ENT < KB, pltpu.roll(wide, KDIM - KB, 1), -pltpu.roll(wide, KB, 1)
    ).astype(jnp.bfloat16)
    spread = spread_ref[...]
    row = lax.broadcasted_iota(jnp.int32, (MIX * SB, KDIM), 0)
    lane = lax.broadcasted_iota(jnp.int32, (MIX * SB, KDIM), 1)
    left = jnp.where(
        row % MIX < MIX // 2,
        jnp.dot(spread, own, preferred_element_type=jnp.float32),
        jnp.dot(spread, turned, preferred_element_type=jnp.float32),
    )
    left = jnp.where(row // NBLK % KB == lane % KB, left, 0.0).astype(jnp.bfloat16)
    cross_ref[...] = lax.dot_general(
        left, met_ref[...], (((1,), (1,)), ((), ())), preferred_element_type=jnp.float32
    )
    for i in range(SB):
        piece = cross_ref[i * MIX : (i + 1) * MIX, :]
        for met in range(SEEN):
            pair_ref[met * MIX : (met + 1) * MIX, i * SB : (i + 1) * SB] = (
                piece[:, met * SB : (met + 1) * SB]
            )
    picked = jnp.dot(
        pick_ref[...], pair_ref[...].astype(jnp.bfloat16), preferred_element_type=jnp.float32
    ).astype(jnp.bfloat16)
    chosen = jnp.dot(picked, choice_ref[...], preferred_element_type=jnp.float32)
    height = ROUNDS // 2 * ENT
    first = lax.broadcasted_iota(jnp.int32, (height, 2 * SHARE), 1) < SHARE
    for b in range(NBLK):
        for d in range(0, N_DAY, 2):
            low = chosen[b * height : (b + 1) * height, d * SHARE : (d + 2) * SHARE]
            high = chosen[
                (NBLK + b) * height : (NBLK + b + 1) * height, d * SHARE : (d + 2) * SHARE
            ]
            even = jnp.where(first, low, pltpu.roll(high, SHARE, 1))
            odd = jnp.where(first, pltpu.roll(low, SHARE, 1), high)
            out_ref[b * N_DAY + d] = even.astype(jnp.bfloat16)
            out_ref[b * N_DAY + d + 1] = odd.astype(jnp.bfloat16)


def lag_kernel(slot_ref, r_ref, lag_ref, out_ref):
    half = ROUNDS // 2
    lag = lag_ref[...]
    for first in range(0, half, STEPS):
        entries = r_ref[:, first * ENT : (first + STEPS) * ENT, :].reshape(
            GROUP * STEPS * ENT, 2 * SHARE
        )
        lagged = jnp.dot(lag, entries, preferred_element_type=jnp.float32)
        lagged = lagged * (1.0 / math.sqrt(NB * DD * N_DAY))
        for step in range(STEPS):
            turned = lagged[step * LAG_ROWS : (step + 1) * LAG_ROWS, :].T
            out_ref[slot_ref[first + step]] = turned[:SHARE, :LAGS]
            out_ref[slot_ref[half + first + step]] = turned[SHARE:, :LAGS]


def params():
    return pltpu.CompilerParams(vmem_limit_bytes=VMEM)


def vmem_specs(count):
    return [pl.BlockSpec(memory_space=pltpu.VMEM)] * count


def shards(records, offsets, pair_order):
    group_axes = ("zr", "xh", "day")
    parts = band_parts()
    spectra = pl.pallas_call(
        spectra_kernel,
        in_specs=[pl.BlockSpec(memory_space=pltpu.HBM)] * 2,
        out_specs=pl.BlockSpec(memory_space=pltpu.VMEM),
        out_shape=jax.ShapeDtypeStruct((GROUP, ENT, SB * DD), jnp.bfloat16),
        scratch_shapes=[
            pltpu.VMEM((SB, DD, NT), jnp.bfloat16),
            pltpu.VMEM(parts.shape, jnp.float32),
            pltpu.VMEM((SB * DD, NT), jnp.bfloat16),
            pltpu.SemaphoreType.DMA((FETCHES + 1,)),
        ],
        compiler_params=pltpu.CompilerParams(vmem_limit_bytes=62 * 1024 * 1024),
        name="spectra",
    )(records, jnp.asarray(parts))

    by_bin = lax.all_to_all(spectra, group_axes, 0, 0, tiled=True).reshape(2 * NB, SB * DD)

    own = pl.pallas_call(
        gather_days_kernel,
        in_specs=vmem_specs(1),
        out_specs=pl.BlockSpec(memory_space=pltpu.VMEM),
        out_shape=jax.ShapeDtypeStruct((NBLK * SB, KDIM), jnp.bfloat16),
        scratch_shapes=[pltpu.VMEM((NBLK * SB, KDIM), jnp.float32)],
        compiler_params=params(),
        name="gather_days",
    )(by_bin)

    def moved(piece, steps):
        pairs = [(source, (source + steps) % GROUPS) for source in range(GROUPS)]
        return lax.ppermute(piece, "zq", pairs)

    met, far = [own], own
    for _ in range(BACK - 1):
        met.append(moved(met[-1], 1))
    for _ in range(2):
        far = moved(far, -(GROUPS - BACK) // 2)
    met.append(far)

    choice = (
        lax.broadcasted_iota(jnp.int32, (PAIRS, PAIRS), 0) == pair_order[None, :]
    ).astype(jnp.bfloat16)

    chosen = pl.pallas_call(
        cross_kernel,
        in_specs=vmem_specs(BACK + 4),
        out_specs=pl.BlockSpec(memory_space=pltpu.VMEM),
        out_shape=jax.ShapeDtypeStruct((GROUP, ROUNDS // 2 * ENT, 2 * SHARE), jnp.bfloat16),
        scratch_shapes=[
            pltpu.VMEM((SEEN * SB, KDIM), jnp.bfloat16),
            pltpu.VMEM((MIX * SB, SEEN * SB), jnp.float32),
            pltpu.VMEM((MIX * SEEN, PAIRS), jnp.float32),
        ],
        compiler_params=params(),
        name="cross",
    )(*met, jnp.asarray(spread_rows()), jnp.asarray(pick_rows()), choice)

    by_pair = lax.all_to_all(chosen, group_axes, 0, 0, tiled=True)

    steps = jnp.arange(ROUNDS, dtype=jnp.int32)
    slots = jnp.sum(
        jnp.where(offsets[None, :] == steps[:, None], steps[None, :], 0), axis=1
    ).astype(jnp.int32)

    lagged = pl.pallas_call(
        lag_kernel,
        in_specs=[pl.BlockSpec(memory_space=pltpu.SMEM)] + vmem_specs(2),
        out_specs=pl.BlockSpec(memory_space=pltpu.VMEM),
        out_shape=jax.ShapeDtypeStruct((ROUNDS, SHARE, LAGS), jnp.float32),
        compiler_params=params(),
        name="lags",
    )(slots, by_pair, jnp.asarray(lag_table()))
    return jnp.transpose(lagged, (0, 2, 1))


def solution(mesh):
    planes = mesh.shape["stn"] // N_HI
    devices = mesh.devices.reshape(planes // ZG, ZG, N_HI, mesh.shape["day"])
    fine = Mesh(devices, ("zq", "zr", "xh", "day"))
    stations = ("zq", "zr", "xh")
    in_specs = (P(stations, "day", None), P(), P())
    out_specs = P(None, None, stations + ("day",))
    return jax.shard_map(
        shards, mesh=fine, in_specs=in_specs, out_specs=out_specs, check_vma=False
    )
```

time: 141 us -> 93.1 us (0.66)
  waiting for transfers between devices: 74.1 us -> 23.8 us
  starting transfers between devices: 16.6 us -> 36.2 us
  between operations: 13.5 us -> 0.13 us
  local copies, waits for them, and re-layouts: 7.2 us -> 0.06 us
  blocking collectives: 17.3 us -> 19.6 us
    all_gather x1 -> x0, waiting for transfers between devices: 62.6 us -> none  [shards(): everyone = lax.all_gather(own, 'zq', axis=0)]
    ppermute x0 -> x5, starting transfers between devices: none -> 28.7 us  [moved(): return lax.ppermute(piece, 'zq', pairs)]
    ppermute x0 -> x5, waiting for transfers between devices: none -> 11.7 us  [moved(): return lax.ppermute(piece, 'zq', pairs)]
    all_to_all x1, starting transfers between devices: 16.6 us -> 7.51 us  [shards(): by_pair = lax.all_to_all(chosen, group_axes, 0, 0, tiled=True)]
    unnamed x18 -> x10, local copies, waits for them, and re-layouts: 6.11 us -> 0.02 us
    all_to_all x1, blocking collectives: 17.3 us -> 19.6 us  [shards(): lax.all_to_all(spectra, group_axes, 0, 0, tiled=True)]
  transfers between devices with their start and end apart: 2 -> 6, of which waited for: 2 -> 4; matrix products, arithmetic and copies ran while one was open for 1% -> 1% of each run, Pallas kernels for 0% -> 0%
where the time goes in v4:
time: 93.1 us; the launch traced here: 92.7 us
  starting transfers between devices  36.2 us (39%)
  waiting for transfers between devices  23.8 us (26%)
  blocking collectives  19.6 us (21%)
  Pallas kernels  12 us (13%)
  other arithmetic  1 us (1%)
    ppermute x5, starting transfers between devices, moved(): return lax.ppermute(piece, 'zq', pairs)  28.7 us
    all_to_all x1, blocking collectives, shards(): lax.all_to_all(spectra, group_axes, 0, 0, tiled=True)  19.6 us
    all_to_all x1, waiting for transfers between devices, shards(): by_pair = lax.all_to_all(chosen, group_axes, 0, 0, tiled=True)  12.1 us
    ppermute x5, waiting for transfers between devices, moved(): return lax.ppermute(piece, 'zq', pairs)  11.7 us
    all_to_all x1, starting transfers between devices, shards(): by_pair = lax.all_to_all(chosen, group_axes, 0, 0, tiled=True)  7.51 us
    pallas_call x1, Pallas kernels, shards(): pl.pallas_call(spectra_kernel, in_specs=[pl.BlockSpec(memory_space=pltpu....  6.24 us
    pallas_call x1, Pallas kernels, shards(): pl.pallas_call(cross_kernel, in_specs=vmem_specs(BACK + 4), out_specs=pl....  3.39 us
    pallas_call x1, Pallas kernels, shards(): pl.pallas_call(lag_kernel, in_specs=[pl.BlockSpec(memory_space=pltpu.SMEM...  2.14 us
  transfers between devices with their start and end apart: 6, of which 4 were waited for; matrix products, arithmetic and copies ran while one was open for 1% of the time, Pallas kernels for 0%

profile of v4, /device:TPU:1, one launch (start us, length us, event | category | flops | bytes accessed | tf_op | source)
XLA Modules:
  0.0 92.7 jit_solution(8829830001703931217)
XLA Ops:
  0.0 0.0 copy-start.1
  0.0 0.0 copy-start.2
  0.0 0.0 copy-start.3
  0.0 6.2 %spectra.1 = bf16[64,4,256]{2,1,0:T(4,128)(2,1)} custom-call(bf16[32,8,6000]{2,1,0:T(8,128)(2,1)} %records_ref.1, f32[560,256]{1,0:T(8,128)} %constant.10.clone.parts_ref), custom_call_target="tpu_custom_call" | custom-call | tf_op jit(solution)/shard_map/spectra/pallas_call | solution.py:227
  6.3 19.6 %all_to_all.10 = bf16[64,4,256]{2,1,0:T(4,128)(2,1)S(1)} all-to-all(bf16[64,4,256]{2,1,0:T(4,128)(2,1)} %spectra.1), channel_id=1, replica_groups=mesh['zq'=8,'zr'=2,'xh'=2,'day'=16] {'zr','xh','day'}, dimensions={0} | all-to-all | bytes 262144 | tf_op jit(solution)/shard_map/all_to_all | solution.py:242
  25.9 0.2 gather_days.1.refs_0_
  26.1 0.0 copy-start.4
  26.1 0.0 copy-start
  26.1 4.3 %collective-permute-start = (bf16[128,512]{1,0:T(8,128)(2,1)S(1)}, bf16[128,512]{1,0:T(8,128)(2,1)S(1)}, u32[]{:S(2)}, u32[]{:S(2)}) collective-permute-start(bf16[128,512]{1,0:T(8,128)(2,1)S(1)} %gather_days.1.refs_0_), channel_id=1, source_target_pairs={{0,64},{64,128},{128,192},{192,256},{256,320},{320,384},{384,448},... | collective-permute-start | bytes 393224 | tf_op jit(solution)/shard_map/ppermute | solution.py:256
  30.4 9.8 %collective-permute-start.3 = (bf16[128,512]{1,0:T(8,128)(2,1)S(1)}, bf16[128,512]{1,0:T(8,128)(2,1)S(1)}, u32[]{:S(2)}, u32[]{:S(2)}) collective-permute-start(bf16[128,512]{1,0:T(8,128)(2,1)S(1)} %gather_days.1.refs_0_), channel_id=1, source_target_pairs={{0,384},{64,448},{128,0},{192,64},{256,128},{320,192},{384,256},{4... | collective-permute-start | bytes 393224 | tf_op jit(solution)/shard_map/ppermute | solution.py:256
  40.2 0.6 collective-permute-done.refs_1_
  40.8 1.9 %collective-permute-start.1 = (bf16[128,512]{1,0:T(8,128)(2,1)S(1)}, bf16[128,512]{1,0:T(8,128)(2,1)S(1)}, u32[]{:S(2)}, u32[]{:S(2)}) collective-permute-start(bf16[128,512]{1,0:T(8,128)(2,1)S(1)} %collective-permute-done.refs_1_), channel_id=1, source_target_pairs={{0,64},{64,128},{128,192},{192,256},{256,320},{320,384},{384,448},... | collective-permute-start | bytes 393224 | tf_op jit(solution)/shard_map/ppermute | solution.py:256
  42.7 5.5 %collective-permute-done.3 = bf16[128,512]{1,0:T(8,128)(2,1)S(1)} collective-permute-done((bf16[128,512]{1,0:T(8,128)(2,1)S(1)}, bf16[128,512]{1,0:T(8,128)(2,1)S(1)}, u32[]{:S(2)}, u32[]{:S(2)}) %collective-permute-start.3) | collective-permute-done | bytes 131104 | tf_op jit(solution)/shard_map/ppermute | solution.py:256
  48.2 7.1 %collective-permute-start.4 = (bf16[128,512]{1,0:T(8,128)(2,1)S(1)}, bf16[128,512]{1,0:T(8,128)(2,1)S(1)}, u32[]{:S(2)}, u32[]{:S(2)}) collective-permute-start(bf16[128,512]{1,0:T(8,128)(2,1)S(1)} %collective-permute-done.3), channel_id=1, source_target_pairs={{0,384},{64,448},{128,0},{192,64},{256,128},{320,192},{384,256},{4... | collective-permute-start | bytes 393224 | tf_op jit(solution)/shard_map/ppermute | solution.py:256
  55.3 0.0 collective-permute-done.1.refs_2_
  55.3 5.6 %collective-permute-start.2 = (bf16[128,512]{1,0:T(8,128)(2,1)S(1)}, bf16[128,512]{1,0:T(8,128)(2,1)S(1)}, u32[]{:S(2)}, u32[]{:S(2)}) collective-permute-start(bf16[128,512]{1,0:T(8,128)(2,1)S(1)} %collective-permute-done.1.refs_2_), channel_id=1, source_target_pairs={{0,64},{64,128},{128,192},{192,256},{256,320},{320,384},{384,448},... | collective-permute-start | bytes 393224 | tf_op jit(solution)/shard_map/ppermute | solution.py:256
  60.9 0.0 copy-done.3
  60.9 0.9 fusion.refs_7_
  61.8 0.0 collective-permute-done.4.refs_4_
  61.8 5.7 %collective-permute-done.2.refs_3_ = bf16[128,512]{1,0:T(8,128)(2,1)S(1)} collective-permute-done((bf16[128,512]{1,0:T(8,128)(2,1)S(1)}, bf16[128,512]{1,0:T(8,128)(2,1)S(1)}, u32[]{:S(2)}, u32[]{:S(2)}) %collective-permute-start.2) | collective-permute-done | bytes 131104 | tf_op jit(solution)/shard_map/ppermute | solution.py:256
  67.5 0.0 copy-done.1
  67.5 0.0 copy-done.2
  67.5 3.4 %cross.1 = bf16[64,32,128]{2,1,0:T(8,128)(2,1)} custom-call(bf16[128,512]{1,0:T(8,128)(2,1)S(1)} %gather_days.1.refs_0_, bf16[128,512]{1,0:T(8,128)(2,1)S(1)} %collective-permute-done.refs_1_, bf16[128,512]{1,0:T(8,128)(2,1)S(1)} %collective-permute-done.1.refs_2_, bf16[128,512]{1,0:T(8,128)(2,1)S(1)} %collective-permute-done.2.refs_3_, ...), custom_call_target="tpu_custom_call" | custom-call | tf_op jit(solution)/shard_map/cross/pallas_call | solution.py:269
  70.9 7.5 %all-to-all-start.1 = ((bf16[64,32,128]{2,1,0:T(8,128)(2,1)}), bf16[64,32,128]{2,1,0:T(8,128)(2,1)S(1)}, u32[]{:S(2)}, u32[]{:S(2)}) async-start(bf16[64,32,128]{2,1,0:T(8,128)(2,1)} %cross.1), calls=%async_computation.1 | async-start | bytes 1048576 | tf_op jit(solution)/shard_map/all_to_all | solution.py:283
  78.4 0.0 copy-done.4
  78.4 0.1 select_reduce_fusion.slot_ref
  78.5 12.1 %all-to-all-done.1.r_ref = bf16[64,32,128]{2,1,0:T(8,128)(2,1)S(1)} async-done(((bf16[64,32,128]{2,1,0:T(8,128)(2,1)}), bf16[64,32,128]{2,1,0:T(8,128)(2,1)S(1)}, u32[]{:S(2)}, u32[]{:S(2)}) %all-to-all-start.1) | async-done | bytes 524320 | tf_op jit(solution)/shard_map/all_to_all | solution.py:283
  90.6 0.0 copy-done
  90.6 2.1 %lags.1 = f32[16,64,101]{2,1,0:T(8,128)} custom-call(s32[16]{0:T(128)S(1)} %select_reduce_fusion.slot_ref, bf16[64,32,128]{2,1,0:T(8,128)(2,1)S(1)} %all-to-all-done.1.r_ref, bf16[512,1024]{1,0:T(8,128)(2,1)S(1)} %copy-done), custom_call_target="tpu_custom_call" | custom-call | tf_op jit(solution)/shard_map/lags/pallas_call | solution.py:290
  (1 shorter events, 0.0 us)
Async XLA Ops:
  0.0 67.5 %copy-start.1 = (bf16[256,320]{1,0:T(8,128)(2,1)S(1)}, bf16[256,320]{1,0:T(8,128)(2,1)}, u32[]{:S(2)}) copy-start(bf16[256,320]{1,0:T(8,128)(2,1)} %constant.12.clone.refs_6_) | copy-start | bytes 491524
  0.0 67.5 %copy-start.2 = (bf16[512,128]{1,0:T(8,128)(2,1)S(1)}, bf16[512,128]{1,0:T(8,128)(2,1)}, u32[]{:S(2)}) copy-start(bf16[512,128]{1,0:T(8,128)(2,1)} %constant.11.clone.refs_5_) | copy-start | bytes 393220
  0.0 60.9 %copy-start.3 = (s32[1024]{0:T(1024)S(1)}, s32[1024]{0:T(1024)}, u32[]{:S(2)}) copy-start(s32[1024]{0:T(1024)} %param.9) | copy-start | bytes 12292
  26.1 52.3 %copy-start.4 = (s32[16]{0:T(128)S(1)}, s32[16]{0:T(128)}, u32[]{:S(2)}) copy-start(s32[16]{0:T(128)} %param.8) | copy-start | bytes 196
  26.1 64.5 %copy-start = (bf16[512,1024]{1,0:T(8,128)(2,1)S(1)}, bf16[512,1024]{1,0:T(8,128)(2,1)}, u32[]{:S(2)}) copy-start(bf16[512,1024]{1,0:T(8,128)(2,1)} %constant.13.clone.lag_ref) | copy-start | bytes 3145732
  26.1 14.7 %collective-permute-start = (bf16[128,512]{1,0:T(8,128)(2,1)S(1)}, bf16[128,512]{1,0:T(8,128)(2,1)S(1)}, u32[]{:S(2)}, u32[]{:S(2)}) collective-permute-start(bf16[128,512]{1,0:T(8,128)(2,1)S(1)} %gather_days.1.refs_0_), channel_id=1, source_target_pairs={{0,64},{64,128},{128,192},{192,256},{256,320},{320,384},{384,448},... | collective-permute-start | bytes 393224 | tf_op jit(solution)/shard_map/ppermute | solution.py:256
  30.4 17.8 %collective-permute-start.3 = (bf16[128,512]{1,0:T(8,128)(2,1)S(1)}, bf16[128,512]{1,0:T(8,128)(2,1)S(1)}, u32[]{:S(2)}, u32[]{:S(2)}) collective-permute-start(bf16[128,512]{1,0:T(8,128)(2,1)S(1)} %gather_days.1.refs_0_), channel_id=1, source_target_pairs={{0,384},{64,448},{128,0},{192,64},{256,128},{320,192},{384,256},{4... | collective-permute-start | bytes 393224 | tf_op jit(solution)/shard_map/ppermute | solution.py:256
  40.8 14.5 %collective-permute-start.1 = (bf16[128,512]{1,0:T(8,128)(2,1)S(1)}, bf16[128,512]{1,0:T(8,128)(2,1)S(1)}, u32[]{:S(2)}, u32[]{:S(2)}) collective-permute-start(bf16[128,512]{1,0:T(8,128)(2,1)S(1)} %collective-permute-done.refs_1_), channel_id=1, source_target_pairs={{0,64},{64,128},{128,192},{192,256},{256,320},{320,384},{384,448},... | collective-permute-start | bytes 393224 | tf_op jit(solution)/shard_map/ppermute | solution.py:256
  48.2 13.6 %collective-permute-start.4 = (bf16[128,512]{1,0:T(8,128)(2,1)S(1)}, bf16[128,512]{1,0:T(8,128)(2,1)S(1)}, u32[]{:S(2)}, u32[]{:S(2)}) collective-permute-start(bf16[128,512]{1,0:T(8,128)(2,1)S(1)} %collective-permute-done.3), channel_id=1, source_target_pairs={{0,384},{64,448},{128,0},{192,64},{256,128},{320,192},{384,256},{4... | collective-permute-start | bytes 393224 | tf_op jit(solution)/shard_map/ppermute | solution.py:256
  55.3 12.2 %collective-permute-start.2 = (bf16[128,512]{1,0:T(8,128)(2,1)S(1)}, bf16[128,512]{1,0:T(8,128)(2,1)S(1)}, u32[]{:S(2)}, u32[]{:S(2)}) collective-permute-start(bf16[128,512]{1,0:T(8,128)(2,1)S(1)} %collective-permute-done.1.refs_2_), channel_id=1, source_target_pairs={{0,64},{64,128},{128,192},{192,256},{256,320},{320,384},{384,448},... | collective-permute-start | bytes 393224 | tf_op jit(solution)/shard_map/ppermute | solution.py:256
  70.9 19.7 %all-to-all-start.1 = ((bf16[64,32,128]{2,1,0:T(8,128)(2,1)}), bf16[64,32,128]{2,1,0:T(8,128)(2,1)S(1)}, u32[]{:S(2)}, u32[]{:S(2)}) async-start(bf16[64,32,128]{2,1,0:T(8,128)(2,1)} %cross.1), calls=%async_computation.1 | async-start | bytes 1048576 | tf_op jit(solution)/shard_map/all_to_all | solution.py:283

commit v5 on v4

--- a/solution.py
+++ b/solution.py
@@ -37,7 +37,8 @@
 LAG_ROWS = 128
 STEPS = 16 // ENT
 BASE = 256
-FETCHES = 8
+PIECE = 1536
+PIECES = [(start, min(PIECE, NT - start)) for start in range(0, NT, PIECE)]
 VMEM = 44 * 1024 * 1024
 
 assert NB == GROUP * KB and ROUNDS == BACK * NBLK
@@ -59,7 +60,10 @@
     coarse = unit * (np.arange(0, NT, BASE)[:, None] * bins % NT)
     with_cos = np.where(imag, -np.sin(coarse), np.cos(coarse))
     with_sin = np.where(imag, -np.cos(coarse), -np.sin(coarse))
-    parts = np.concatenate([np.cos(fine), np.sin(fine), with_cos, with_sin], axis=0)
+    real, imag = phase_table(np.arange(NT, dtype=np.int64))
+    sums = np.stack([real.reshape(GROUP, KB, NT), imag.reshape(GROUP, KB, NT)], axis=1)
+    sums = sums.astype(np.float64).sum(axis=3).reshape(1, 2 * NB)
+    parts = np.concatenate([np.cos(fine), np.sin(fine), with_cos, with_sin, sums], axis=0)
     return np.pad(parts, ((0, -len(parts) % 8), (0, 0))).astype(np.float32)
 
 
@@ -95,38 +99,55 @@
     return table
 
 
-def spectra_kernel(records_ref, parts_ref, out_ref, x_ref, angle_ref, centred_ref, sems):
-    part = SB // FETCHES
+def spectra_kernel(records_ref, parts_ref, out_ref, x_ref, angle_ref, sems):
     copies = [
         pltpu.make_async_copy(
-            records_ref.at[pl.ds(i * part, part)], x_ref.at[pl.ds(i * part, part)], sems.at[i]
+            records_ref.at[:, :, pl.ds(start, size)], x_ref.at[:, :, pl.ds(start, size)], sems.at[i]
         )
-        for i in range(FETCHES)
+        for i, (start, size) in enumerate(PIECES)
     ]
-    angles = pltpu.make_async_copy(parts_ref, angle_ref, sems.at[FETCHES])
+    angles = pltpu.make_async_copy(parts_ref, angle_ref, sems.at[len(PIECES)])
+    copies[0].start()
     angles.start()
-    for copy in copies:
+    for copy in copies[1:]:
         copy.start()
-    powers = []
-    for i, copy in enumerate(copies):
-        copy.wait()
-        x = x_ref[i * part : (i + 1) * part].astype(jnp.float32).reshape(part * DD, NT)
-        x = x - jnp.sum(x, axis=1, keepdims=True) * (1.0 / NT)
-        powers.append(jnp.sum(x * x, axis=1, keepdims=True) * (1.0 / NT))
-        centred_ref[i * part * DD : (i + 1) * part * DD, :] = x.astype(jnp.bfloat16)
-    power = jnp.concatenate(powers, axis=0)
-    angles.wait()
+
+    def samples(start, size):
+        return x_ref[:, :, start : start + size].astype(jnp.float32).reshape(SB * DD, size)
+
     blocks = pl.cdiv(NT, BASE)
     raw = jnp.zeros((SB * DD, 2 * NB), jnp.float32)
-    for block in range(blocks):
-        start, size = block * BASE, min(BASE, NT - block * BASE)
-        with_cos = angle_ref[2 * BASE + block : 2 * BASE + block + 1, :]
-        with_sin = angle_ref[2 * BASE + blocks + block : 2 * BASE + blocks + block + 1, :]
-        table = with_cos * angle_ref[:size, :] + with_sin * angle_ref[BASE : BASE + size, :]
-        raw = raw + jnp.dot(
-            centred_ref[:, start : start + size], table.astype(jnp.bfloat16),
-            preferred_element_type=jnp.float32,
-        )
+    lanes = BASE // 2
+    totals = jnp.zeros((SB * DD, lanes), jnp.float32)
+    squares = jnp.zeros((SB * DD, lanes), jnp.float32)
+    total = square = 0.0
+    for i, (begin, length) in enumerate(PIECES):
+        copies[i].wait()
+        if i == 0:
+            first_mean = jnp.sum(samples(begin, length), axis=1, keepdims=True) * (1.0 / length)
+            angles.wait()
+        for start in range(begin, begin + length, BASE):
+            block, size = start // BASE, min(BASE, NT - start)
+            with_cos = angle_ref[2 * BASE + block : 2 * BASE + block + 1, :]
+            with_sin = angle_ref[2 * BASE + blocks + block : 2 * BASE + blocks + block + 1, :]
+            table = with_cos * angle_ref[:size, :] + with_sin * angle_ref[BASE : BASE + size, :]
+            x = samples(start, size) - first_mean
+            if size == BASE:
+                low, high = x[:, :lanes], x[:, lanes:]
+                totals = totals + (low + high)
+                squares = squares + (low * low + high * high)
+            else:
+                total = total + jnp.sum(x, axis=1, keepdims=True)
+                square = square + jnp.sum(x * x, axis=1, keepdims=True)
+            raw = raw + jnp.dot(
+                x.astype(jnp.bfloat16), table.astype(jnp.bfloat16),
+                preferred_element_type=jnp.float32,
+            )
+    total = total + jnp.sum(totals, axis=1, keepdims=True)
+    square = square + jnp.sum(squares, axis=1, keepdims=True)
+    rest = total * (1.0 / NT)
+    raw = raw - rest * angle_ref[2 * BASE + 2 * blocks : 2 * BASE + 2 * blocks + 1, :]
+    power = jnp.maximum(square * (1.0 / NT) - rest * rest, 0.0)
     raw = raw / jnp.sqrt(power + 1e-06)
     scale = jnp.sqrt(jnp.sum(raw * raw, axis=1, keepdims=True) * (1.0 / NB) + 1e-06)
     spectra = (raw / scale).astype(jnp.bfloat16)
@@ -232,8 +253,7 @@
         scratch_shapes=[
             pltpu.VMEM((SB, DD, NT), jnp.bfloat16),
             pltpu.VMEM(parts.shape, jnp.float32),
-            pltpu.VMEM((SB * DD, NT), jnp.bfloat16),
-            pltpu.SemaphoreType.DMA((FETCHES + 1,)),
+            pltpu.SemaphoreType.DMA((len(PIECES) + 1,)),
         ],
         compiler_params=pltpu.CompilerParams(vmem_limit_bytes=62 * 1024 * 1024),
         name="spectra",

time: 93.1 us -> 91.7 us (0.985)
  Pallas kernels: 12 us -> 10.6 us
    pallas_call x1, Pallas kernels: 6.24 us -> 4.82 us  [shards(): pl.pallas_call(spectra_kernel, in_specs=[pl.BlockSpec(memory_space=pltpu....]
where the time goes in v5:
time: 91.7 us; the launch traced here: 91.3 us
  starting transfers between devices  36.2 us (39%)
  waiting for transfers between devices  23.8 us (26%)
  blocking collectives  19.6 us (21%)
  Pallas kernels  10.6 us (12%)
  other arithmetic  1 us (1%)
    ppermute x5, starting transfers between devices, moved(): return lax.ppermute(piece, 'zq', pairs)  28.7 us
    all_to_all x1, blocking collectives, shards(): lax.all_to_all(spectra, group_axes, 0, 0, tiled=True)  19.6 us
    all_to_all x1, waiting for transfers between devices, shards(): by_pair = lax.all_to_all(chosen, group_axes, 0, 0, tiled=True)  12.1 us
    ppermute x5, waiting for transfers between devices, moved(): return lax.ppermute(piece, 'zq', pairs)  11.7 us
    all_to_all x1, starting transfers between devices, shards(): by_pair = lax.all_to_all(chosen, group_axes, 0, 0, tiled=True)  7.52 us
    pallas_call x1, Pallas kernels, shards(): pl.pallas_call(spectra_kernel, in_specs=[pl.BlockSpec(memory_space=pltpu....  4.82 us
    pallas_call x1, Pallas kernels, shards(): pl.pallas_call(cross_kernel, in_specs=vmem_specs(BACK + 4), out_specs=pl....  3.4 us
    pallas_call x1, Pallas kernels, shards(): pl.pallas_call(lag_kernel, in_specs=[pl.BlockSpec(memory_space=pltpu.SMEM...  2.14 us
  transfers between devices with their start and end apart: 6, of which 4 were waited for; matrix products, arithmetic and copies ran while one was open for 1% of the time, Pallas kernels for 0%

profile of v5, /device:TPU:1, one launch (start us, length us, event | category | flops | bytes accessed | tf_op | source)
XLA Modules:
  0.0 91.3 jit_solution(13914004875321892881)
XLA Ops:
  0.0 0.0 copy-start.1
  0.0 0.0 copy-start.2
  0.0 0.0 copy-start.3
  0.0 4.8 %spectra.1 = bf16[64,4,256]{2,1,0:T(4,128)(2,1)} custom-call(bf16[32,8,6000]{2,1,0:T(8,128)(2,1)} %records_ref.1, f32[568,256]{1,0:T(8,128)} %constant.10.clone.parts_ref), custom_call_target="tpu_custom_call" | custom-call | tf_op jit(solution)/shard_map/spectra/pallas_call | solution.py:248
  4.8 19.6 %all_to_all.10 = bf16[64,4,256]{2,1,0:T(4,128)(2,1)S(1)} all-to-all(bf16[64,4,256]{2,1,0:T(4,128)(2,1)} %spectra.1), channel_id=1, replica_groups=mesh['zq'=8,'zr'=2,'xh'=2,'day'=16] {'zr','xh','day'}, dimensions={0} | all-to-all | bytes 262144 | tf_op jit(solution)/shard_map/all_to_all | solution.py:262
  24.5 0.2 gather_days.1.refs_0_
  24.7 0.0 copy-start.4
  24.7 0.0 copy-start
  24.7 4.3 %collective-permute-start = (bf16[128,512]{1,0:T(8,128)(2,1)S(1)}, bf16[128,512]{1,0:T(8,128)(2,1)S(1)}, u32[]{:S(2)}, u32[]{:S(2)}) collective-permute-start(bf16[128,512]{1,0:T(8,128)(2,1)S(1)} %gather_days.1.refs_0_), channel_id=1, source_target_pairs={{0,64},{64,128},{128,192},{192,256},{256,320},{320,384},{384,448},... | collective-permute-start | bytes 393224 | tf_op jit(solution)/shard_map/ppermute | solution.py:276
  29.0 9.8 %collective-permute-start.3 = (bf16[128,512]{1,0:T(8,128)(2,1)S(1)}, bf16[128,512]{1,0:T(8,128)(2,1)S(1)}, u32[]{:S(2)}, u32[]{:S(2)}) collective-permute-start(bf16[128,512]{1,0:T(8,128)(2,1)S(1)} %gather_days.1.refs_0_), channel_id=1, source_target_pairs={{0,384},{64,448},{128,0},{192,64},{256,128},{320,192},{384,256},{4... | collective-permute-start | bytes 393224 | tf_op jit(solution)/shard_map/ppermute | solution.py:276
  38.8 0.6 collective-permute-done.refs_1_
  39.4 1.9 %collective-permute-start.1 = (bf16[128,512]{1,0:T(8,128)(2,1)S(1)}, bf16[128,512]{1,0:T(8,128)(2,1)S(1)}, u32[]{:S(2)}, u32[]{:S(2)}) collective-permute-start(bf16[128,512]{1,0:T(8,128)(2,1)S(1)} %collective-permute-done.refs_1_), channel_id=1, source_target_pairs={{0,64},{64,128},{128,192},{192,256},{256,320},{320,384},{384,448},... | collective-permute-start | bytes 393224 | tf_op jit(solution)/shard_map/ppermute | solution.py:276
  41.3 5.5 %collective-permute-done.3 = bf16[128,512]{1,0:T(8,128)(2,1)S(1)} collective-permute-done((bf16[128,512]{1,0:T(8,128)(2,1)S(1)}, bf16[128,512]{1,0:T(8,128)(2,1)S(1)}, u32[]{:S(2)}, u32[]{:S(2)}) %collective-permute-start.3) | collective-permute-done | bytes 131104 | tf_op jit(solution)/shard_map/ppermute | solution.py:276
  46.8 7.1 %collective-permute-start.4 = (bf16[128,512]{1,0:T(8,128)(2,1)S(1)}, bf16[128,512]{1,0:T(8,128)(2,1)S(1)}, u32[]{:S(2)}, u32[]{:S(2)}) collective-permute-start(bf16[128,512]{1,0:T(8,128)(2,1)S(1)} %collective-permute-done.3), channel_id=1, source_target_pairs={{0,384},{64,448},{128,0},{192,64},{256,128},{320,192},{384,256},{4... | collective-permute-start | bytes 393224 | tf_op jit(solution)/shard_map/ppermute | solution.py:276
  53.9 0.0 collective-permute-done.1.refs_2_
  53.9 5.6 %collective-permute-start.2 = (bf16[128,512]{1,0:T(8,128)(2,1)S(1)}, bf16[128,512]{1,0:T(8,128)(2,1)S(1)}, u32[]{:S(2)}, u32[]{:S(2)}) collective-permute-start(bf16[128,512]{1,0:T(8,128)(2,1)S(1)} %collective-permute-done.1.refs_2_), channel_id=1, source_target_pairs={{0,64},{64,128},{128,192},{192,256},{256,320},{320,384},{384,448},... | collective-permute-start | bytes 393224 | tf_op jit(solution)/shard_map/ppermute | solution.py:276
  59.5 0.0 copy-done.3
  59.5 0.9 fusion.refs_7_
  60.4 0.0 collective-permute-done.4.refs_4_
  60.4 5.6 %collective-permute-done.2.refs_3_ = bf16[128,512]{1,0:T(8,128)(2,1)S(1)} collective-permute-done((bf16[128,512]{1,0:T(8,128)(2,1)S(1)}, bf16[128,512]{1,0:T(8,128)(2,1)S(1)}, u32[]{:S(2)}, u32[]{:S(2)}) %collective-permute-start.2) | collective-permute-done | bytes 131104 | tf_op jit(solution)/shard_map/ppermute | solution.py:276
  66.1 0.0 copy-done.1
  66.1 0.0 copy-done.2
  66.1 3.4 %cross.1 = bf16[64,32,128]{2,1,0:T(8,128)(2,1)} custom-call(bf16[128,512]{1,0:T(8,128)(2,1)S(1)} %gather_days.1.refs_0_, bf16[128,512]{1,0:T(8,128)(2,1)S(1)} %collective-permute-done.refs_1_, bf16[128,512]{1,0:T(8,128)(2,1)S(1)} %collective-permute-done.1.refs_2_, bf16[128,512]{1,0:T(8,128)(2,1)S(1)} %collective-permute-done.2.refs_3_, ...), custom_call_target="tpu_custom_call" | custom-call | tf_op jit(solution)/shard_map/cross/pallas_call | solution.py:289
  69.5 7.5 %all-to-all-start.1 = ((bf16[64,32,128]{2,1,0:T(8,128)(2,1)}), bf16[64,32,128]{2,1,0:T(8,128)(2,1)S(1)}, u32[]{:S(2)}, u32[]{:S(2)}) async-start(bf16[64,32,128]{2,1,0:T(8,128)(2,1)} %cross.1), calls=%async_computation.1 | async-start | bytes 1048576 | tf_op jit(solution)/shard_map/all_to_all | solution.py:303
  77.0 0.0 copy-done.4
  77.0 0.1 select_reduce_fusion.slot_ref
  77.1 12.1 %all-to-all-done.1.r_ref = bf16[64,32,128]{2,1,0:T(8,128)(2,1)S(1)} async-done(((bf16[64,32,128]{2,1,0:T(8,128)(2,1)}), bf16[64,32,128]{2,1,0:T(8,128)(2,1)S(1)}, u32[]{:S(2)}, u32[]{:S(2)}) %all-to-all-start.1) | async-done | bytes 524320 | tf_op jit(solution)/shard_map/all_to_all | solution.py:303
  89.2 0.0 copy-done
  89.2 2.1 %lags.1 = f32[16,64,101]{2,1,0:T(8,128)} custom-call(s32[16]{0:T(128)S(1)} %select_reduce_fusion.slot_ref, bf16[64,32,128]{2,1,0:T(8,128)(2,1)S(1)} %all-to-all-done.1.r_ref, bf16[512,1024]{1,0:T(8,128)(2,1)S(1)} %copy-done), custom_call_target="tpu_custom_call" | custom-call | tf_op jit(solution)/shard_map/lags/pallas_call | solution.py:310
  (1 shorter events, 0.0 us)
Async XLA Ops:
  0.0 66.1 %copy-start.1 = (bf16[256,320]{1,0:T(8,128)(2,1)S(1)}, bf16[256,320]{1,0:T(8,128)(2,1)}, u32[]{:S(2)}) copy-start(bf16[256,320]{1,0:T(8,128)(2,1)} %constant.12.clone.refs_6_) | copy-start | bytes 491524
  0.0 66.1 %copy-start.2 = (bf16[512,128]{1,0:T(8,128)(2,1)S(1)}, bf16[512,128]{1,0:T(8,128)(2,1)}, u32[]{:S(2)}) copy-start(bf16[512,128]{1,0:T(8,128)(2,1)} %constant.11.clone.refs_5_) | copy-start | bytes 393220
  0.0 59.5 %copy-start.3 = (s32[1024]{0:T(1024)S(1)}, s32[1024]{0:T(1024)}, u32[]{:S(2)}) copy-start(s32[1024]{0:T(1024)} %param.9) | copy-start | bytes 12292
  24.7 52.3 %copy-start.4 = (s32[16]{0:T(128)S(1)}, s32[16]{0:T(128)}, u32[]{:S(2)}) copy-start(s32[16]{0:T(128)} %param.8) | copy-start | bytes 196
  24.7 64.5 %copy-start = (bf16[512,1024]{1,0:T(8,128)(2,1)S(1)}, bf16[512,1024]{1,0:T(8,128)(2,1)}, u32[]{:S(2)}) copy-start(bf16[512,1024]{1,0:T(8,128)(2,1)} %constant.13.clone.lag_ref) | copy-start | bytes 3145732
  24.7 14.7 %collective-permute-start = (bf16[128,512]{1,0:T(8,128)(2,1)S(1)}, bf16[128,512]{1,0:T(8,128)(2,1)S(1)}, u32[]{:S(2)}, u32[]{:S(2)}) collective-permute-start(bf16[128,512]{1,0:T(8,128)(2,1)S(1)} %gather_days.1.refs_0_), channel_id=1, source_target_pairs={{0,64},{64,128},{128,192},{192,256},{256,320},{320,384},{384,448},... | collective-permute-start | bytes 393224 | tf_op jit(solution)/shard_map/ppermute | solution.py:276
  29.0 17.8 %collective-permute-start.3 = (bf16[128,512]{1,0:T(8,128)(2,1)S(1)}, bf16[128,512]{1,0:T(8,128)(2,1)S(1)}, u32[]{:S(2)}, u32[]{:S(2)}) collective-permute-start(bf16[128,512]{1,0:T(8,128)(2,1)S(1)} %gather_days.1.refs_0_), channel_id=1, source_target_pairs={{0,384},{64,448},{128,0},{192,64},{256,128},{320,192},{384,256},{4... | collective-permute-start | bytes 393224 | tf_op jit(solution)/shard_map/ppermute | solution.py:276
  39.4 14.5 %collective-permute-start.1 = (bf16[128,512]{1,0:T(8,128)(2,1)S(1)}, bf16[128,512]{1,0:T(8,128)(2,1)S(1)}, u32[]{:S(2)}, u32[]{:S(2)}) collective-permute-start(bf16[128,512]{1,0:T(8,128)(2,1)S(1)} %collective-permute-done.refs_1_), channel_id=1, source_target_pairs={{0,64},{64,128},{128,192},{192,256},{256,320},{320,384},{384,448},... | collective-permute-start | bytes 393224 | tf_op jit(solution)/shard_map/ppermute | solution.py:276
  46.8 13.6 %collective-permute-start.4 = (bf16[128,512]{1,0:T(8,128)(2,1)S(1)}, bf16[128,512]{1,0:T(8,128)(2,1)S(1)}, u32[]{:S(2)}, u32[]{:S(2)}) collective-permute-start(bf16[128,512]{1,0:T(8,128)(2,1)S(1)} %collective-permute-done.3), channel_id=1, source_target_pairs={{0,384},{64,448},{128,0},{192,64},{256,128},{320,192},{384,256},{4... | collective-permute-start | bytes 393224 | tf_op jit(solution)/shard_map/ppermute | solution.py:276
  53.9 12.1 %collective-permute-start.2 = (bf16[128,512]{1,0:T(8,128)(2,1)S(1)}, bf16[128,512]{1,0:T(8,128)(2,1)S(1)}, u32[]{:S(2)}, u32[]{:S(2)}) collective-permute-start(bf16[128,512]{1,0:T(8,128)(2,1)S(1)} %collective-permute-done.1.refs_2_), channel_id=1, source_target_pairs={{0,64},{64,128},{128,192},{192,256},{256,320},{320,384},{384,448},... | collective-permute-start | bytes 393224 | tf_op jit(solution)/shard_map/ppermute | solution.py:276
  69.5 19.7 %all-to-all-start.1 = ((bf16[64,32,128]{2,1,0:T(8,128)(2,1)}), bf16[64,32,128]{2,1,0:T(8,128)(2,1)S(1)}, u32[]{:S(2)}, u32[]{:S(2)}) async-start(bf16[64,32,128]{2,1,0:T(8,128)(2,1)} %cross.1), calls=%async_computation.1 | async-start | bytes 1048576 | tf_op jit(solution)/shard_map/all_to_all | solution.py:303

commit v6 on v5

--- a/solution.py
+++ b/solution.py
@@ -175,7 +175,7 @@
     group_refs = refs[: BACK + 1]
     spread_ref, pick_ref, choice_ref, out_ref, met_ref, cross_ref, pair_ref = refs[BACK + 1 :]
     for step, group_ref in enumerate(group_refs):
-        start = (BACK - step) * NBLK * SB
+        start = step * NBLK * SB
         met_ref[start : start + NBLK * SB, :] = group_ref[...]
     own = met_ref[BACK * NBLK * SB :, :]
     wide = own.astype(jnp.float32)
@@ -219,8 +219,9 @@
             out_ref[b * N_DAY + d + 1] = odd.astype(jnp.bfloat16)
 
 
-def lag_kernel(slot_ref, r_ref, lag_ref, out_ref):
+def lag_kernel(slot_ref, r_ref, lag_ref, out_ref, made_ref, sems):
     half = ROUNDS // 2
+    copies = []
     lag = lag_ref[...]
     for first in range(0, half, STEPS):
         entries = r_ref[:, first * ENT : (first + STEPS) * ENT, :].reshape(
@@ -230,8 +231,19 @@
         lagged = lagged * (1.0 / math.sqrt(NB * DD * N_DAY))
         for step in range(STEPS):
             turned = lagged[step * LAG_ROWS : (step + 1) * LAG_ROWS, :].T
-            out_ref[slot_ref[first + step]] = turned[:SHARE, :LAGS]
-            out_ref[slot_ref[half + first + step]] = turned[SHARE:, :LAGS]
+            for round_step, part in (
+                (first + step, turned[:SHARE, :LAGS]),
+                (half + first + step, turned[SHARE:, :LAGS]),
+            ):
+                made_ref[round_step] = part
+                copies.append(
+                    pltpu.make_async_copy(
+                        made_ref.at[round_step], out_ref.at[slot_ref[round_step]], sems.at[round_step]
+                    )
+                )
+                copies[-1].start()
+    for copy in copies:
+        copy.wait()
 
 
 def params():
@@ -275,11 +287,11 @@
         pairs = [(source, (source + steps) % GROUPS) for source in range(GROUPS)]
         return lax.ppermute(piece, "zq", pairs)
 
-    met, far = [own], own
-    for _ in range(BACK - 1):
+    half_way = moved(own, -(GROUPS - BACK) // 2)
+    met = [own, moved(own, 1)]
+    far = moved(half_way, -(GROUPS - BACK) // 2)
+    for _ in range(BACK - 2):
         met.append(moved(met[-1], 1))
-    for _ in range(2):
-        far = moved(far, -(GROUPS - BACK) // 2)
     met.append(far)
 
     choice = (
@@ -298,7 +310,7 @@
         ],
         compiler_params=params(),
         name="cross",
-    )(*met, jnp.asarray(spread_rows()), jnp.asarray(pick_rows()), choice)
+    )(*reversed(met), jnp.asarray(spread_rows()), jnp.asarray(pick_rows()), choice)
 
     by_pair = lax.all_to_all(chosen, group_axes, 0, 0, tiled=True)
 
@@ -310,8 +322,12 @@
     lagged = pl.pallas_call(
         lag_kernel,
         in_specs=[pl.BlockSpec(memory_space=pltpu.SMEM)] + vmem_specs(2),
-        out_specs=pl.BlockSpec(memory_space=pltpu.VMEM),
+        out_specs=pl.BlockSpec(memory_space=pltpu.HBM),
         out_shape=jax.ShapeDtypeStruct((ROUNDS, SHARE, LAGS), jnp.float32),
+        scratch_shapes=[
+            pltpu.VMEM((ROUNDS, SHARE, LAGS), jnp.float32),
+            pltpu.SemaphoreType.DMA((ROUNDS,)),
+        ],
         compiler_params=params(),
         name="lags",
     )(slots, by_pair, jnp.asarray(lag_table()))

time: 91.7 us -> 91.7 us (level)
  no operation moved by 1% of the time
where the time goes in v6:
time: 91.7 us; the launch traced here: 91.3 us
  starting transfers between devices  36.2 us (39%)
  waiting for transfers between devices  23.8 us (26%)
  blocking collectives  19.6 us (21%)
  Pallas kernels  10.6 us (12%)
  other arithmetic  1 us (1%)
    ppermute x5, starting transfers between devices, moved(): return lax.ppermute(piece, 'zq', pairs)  28.7 us
    all_to_all x1, blocking collectives, shards(): lax.all_to_all(spectra, group_axes, 0, 0, tiled=True)  19.6 us
    all_to_all x1, waiting for transfers between devices, shards(): by_pair = lax.all_to_all(chosen, group_axes, 0, 0, tiled=True)  12.1 us
    ppermute x5, waiting for transfers between devices, moved(): return lax.ppermute(piece, 'zq', pairs)  11.7 us
    all_to_all x1, starting transfers between devices, shards(): by_pair = lax.all_to_all(chosen, group_axes, 0, 0, tiled=True)  7.52 us
    pallas_call x1, Pallas kernels, shards(): pl.pallas_call(spectra_kernel, in_specs=[pl.BlockSpec(memory_space=pltpu....  4.82 us
    pallas_call x1, Pallas kernels, shards(): pl.pallas_call(cross_kernel, in_specs=vmem_specs(BACK + 4), out_specs=pl....  3.4 us
    pallas_call x1, Pallas kernels, shards(): pl.pallas_call(lag_kernel, in_specs=[pl.BlockSpec(memory_space=pltpu.SMEM...  2.16 us
  transfers between devices with their start and end apart: 6, of which 4 were waited for; matrix products, arithmetic and copies ran while one was open for 1% of the time, Pallas kernels for 0%

profile of v6, /device:TPU:1, one launch (start us, length us, event | category | flops | bytes accessed | tf_op | source)
XLA Modules:
  0.0 91.3 jit_solution(16106434384371040149)
XLA Ops:
  0.0 0.0 copy-start.1
  0.0 0.0 copy-start.2
  0.0 0.0 copy-start.3
  0.0 4.8 %spectra.1 = bf16[64,4,256]{2,1,0:T(4,128)(2,1)} custom-call(bf16[32,8,6000]{2,1,0:T(8,128)(2,1)} %records_ref.1, f32[568,256]{1,0:T(8,128)} %constant.10.clone.parts_ref), custom_call_target="tpu_custom_call" | custom-call | tf_op jit(solution)/shard_map/spectra/pallas_call | solution.py:260
  4.8 19.6 %all_to_all.10 = bf16[64,4,256]{2,1,0:T(4,128)(2,1)S(1)} all-to-all(bf16[64,4,256]{2,1,0:T(4,128)(2,1)} %spectra.1), channel_id=1, replica_groups=mesh['zq'=8,'zr'=2,'xh'=2,'day'=16] {'zr','xh','day'}, dimensions={0} | all-to-all | bytes 262144 | tf_op jit(solution)/shard_map/all_to_all | solution.py:274
  24.5 0.2 gather_days.1.refs_4_
  24.7 0.0 copy-start.4
  24.7 0.0 copy-start
  24.7 4.3 %collective-permute-start.2 = (bf16[128,512]{1,0:T(8,128)(2,1)S(1)}, bf16[128,512]{1,0:T(8,128)(2,1)S(1)}, u32[]{:S(2)}, u32[]{:S(2)}) collective-permute-start(bf16[128,512]{1,0:T(8,128)(2,1)S(1)} %gather_days.1.refs_4_), channel_id=1, source_target_pairs={{0,64},{64,128},{128,192},{192,256},{256,320},{320,384},{384,448},... | collective-permute-start | bytes 393224 | tf_op jit(solution)/shard_map/ppermute | solution.py:288
  29.0 9.8 %collective-permute-start = (bf16[128,512]{1,0:T(8,128)(2,1)S(1)}, bf16[128,512]{1,0:T(8,128)(2,1)S(1)}, u32[]{:S(2)}, u32[]{:S(2)}) collective-permute-start(bf16[128,512]{1,0:T(8,128)(2,1)S(1)} %gather_days.1.refs_4_), channel_id=1, source_target_pairs={{0,384},{64,448},{128,0},{192,64},{256,128},{320,192},{384,256},{4... | collective-permute-start | bytes 393224 | tf_op jit(solution)/shard_map/ppermute | solution.py:288
  38.8 0.6 collective-permute-done.2.refs_3_
  39.4 1.9 %collective-permute-start.3 = (bf16[128,512]{1,0:T(8,128)(2,1)S(1)}, bf16[128,512]{1,0:T(8,128)(2,1)S(1)}, u32[]{:S(2)}, u32[]{:S(2)}) collective-permute-start(bf16[128,512]{1,0:T(8,128)(2,1)S(1)} %collective-permute-done.2.refs_3_), channel_id=1, source_target_pairs={{0,64},{64,128},{128,192},{192,256},{256,320},{320,384},{384,448},... | collective-permute-start | bytes 393224 | tf_op jit(solution)/shard_map/ppermute | solution.py:288
  41.3 5.5 %collective-permute-done = bf16[128,512]{1,0:T(8,128)(2,1)S(1)} collective-permute-done((bf16[128,512]{1,0:T(8,128)(2,1)S(1)}, bf16[128,512]{1,0:T(8,128)(2,1)S(1)}, u32[]{:S(2)}, u32[]{:S(2)}) %collective-permute-start) | collective-permute-done | bytes 131104 | tf_op jit(solution)/shard_map/ppermute | solution.py:288
  46.8 7.1 %collective-permute-start.1 = (bf16[128,512]{1,0:T(8,128)(2,1)S(1)}, bf16[128,512]{1,0:T(8,128)(2,1)S(1)}, u32[]{:S(2)}, u32[]{:S(2)}) collective-permute-start(bf16[128,512]{1,0:T(8,128)(2,1)S(1)} %collective-permute-done), channel_id=1, source_target_pairs={{0,384},{64,448},{128,0},{192,64},{256,128},{320,192},{384,256},{4... | collective-permute-start | bytes 393224 | tf_op jit(solution)/shard_map/ppermute | solution.py:288
  53.9 0.0 collective-permute-done.3.refs_2_
  53.9 5.6 %collective-permute-start.4 = (bf16[128,512]{1,0:T(8,128)(2,1)S(1)}, bf16[128,512]{1,0:T(8,128)(2,1)S(1)}, u32[]{:S(2)}, u32[]{:S(2)}) collective-permute-start(bf16[128,512]{1,0:T(8,128)(2,1)S(1)} %collective-permute-done.3.refs_2_), channel_id=1, source_target_pairs={{0,64},{64,128},{128,192},{192,256},{256,320},{320,384},{384,448},... | collective-permute-start | bytes 393224 | tf_op jit(solution)/shard_map/ppermute | solution.py:288
  59.5 0.0 copy-done.3
  59.5 0.9 fusion.refs_7_
  60.4 0.0 collective-permute-done.1.refs_0_
  60.4 5.6 %collective-permute-done.4.refs_1_ = bf16[128,512]{1,0:T(8,128)(2,1)S(1)} collective-permute-done((bf16[128,512]{1,0:T(8,128)(2,1)S(1)}, bf16[128,512]{1,0:T(8,128)(2,1)S(1)}, u32[]{:S(2)}, u32[]{:S(2)}) %collective-permute-start.4) | collective-permute-done | bytes 131104 | tf_op jit(solution)/shard_map/ppermute | solution.py:288
  66.1 0.0 copy-done.1
  66.1 0.0 copy-done.2
  66.1 3.4 %cross.1 = bf16[64,32,128]{2,1,0:T(8,128)(2,1)} custom-call(bf16[128,512]{1,0:T(8,128)(2,1)S(1)} %collective-permute-done.1.refs_0_, bf16[128,512]{1,0:T(8,128)(2,1)S(1)} %collective-permute-done.4.refs_1_, bf16[128,512]{1,0:T(8,128)(2,1)S(1)} %collective-permute-done.3.refs_2_, bf16[128,512]{1,0:T(8,128)(2,1)S(1)} %collective-permute-done.2.refs_3_, ...), custom_call_target="tpu_custom_call" | custom-call | tf_op jit(solution)/shard_map/cross/pallas_call | solution.py:301
  69.5 7.5 %all-to-all-start.1 = ((bf16[64,32,128]{2,1,0:T(8,128)(2,1)}), bf16[64,32,128]{2,1,0:T(8,128)(2,1)S(1)}, u32[]{:S(2)}, u32[]{:S(2)}) async-start(bf16[64,32,128]{2,1,0:T(8,128)(2,1)} %cross.1), calls=%async_computation.1 | async-start | bytes 1048576 | tf_op jit(solution)/shard_map/all_to_all | solution.py:315
  77.0 0.0 copy-done.4
  77.0 0.1 select_reduce_fusion.slot_ref
  77.1 12.1 %all-to-all-done.1.r_ref = bf16[64,32,128]{2,1,0:T(8,128)(2,1)S(1)} async-done(((bf16[64,32,128]{2,1,0:T(8,128)(2,1)}), bf16[64,32,128]{2,1,0:T(8,128)(2,1)S(1)}, u32[]{:S(2)}, u32[]{:S(2)}) %all-to-all-start.1) | async-done | bytes 524320 | tf_op jit(solution)/shard_map/all_to_all | solution.py:315
  89.2 0.0 copy-done
  89.2 2.2 %lags.1 = f32[16,64,101]{2,1,0:T(8,128)} custom-call(s32[16]{0:T(128)S(1)} %select_reduce_fusion.slot_ref, bf16[64,32,128]{2,1,0:T(8,128)(2,1)S(1)} %all-to-all-done.1.r_ref, bf16[512,1024]{1,0:T(8,128)(2,1)S(1)} %copy-done), custom_call_target="tpu_custom_call" | custom-call | tf_op jit(solution)/shard_map/lags/pallas_call | solution.py:322
  (1 shorter events, 0.0 us)
Async XLA Ops:
  0.0 66.1 %copy-start.1 = (bf16[256,320]{1,0:T(8,128)(2,1)S(1)}, bf16[256,320]{1,0:T(8,128)(2,1)}, u32[]{:S(2)}) copy-start(bf16[256,320]{1,0:T(8,128)(2,1)} %constant.12.clone.refs_6_) | copy-start | bytes 491524
  0.0 66.1 %copy-start.2 = (bf16[512,128]{1,0:T(8,128)(2,1)S(1)}, bf16[512,128]{1,0:T(8,128)(2,1)}, u32[]{:S(2)}) copy-start(bf16[512,128]{1,0:T(8,128)(2,1)} %constant.11.clone.refs_5_) | copy-start | bytes 393220
  0.0 59.5 %copy-start.3 = (s32[1024]{0:T(1024)S(1)}, s32[1024]{0:T(1024)}, u32[]{:S(2)}) copy-start(s32[1024]{0:T(1024)} %param.9) | copy-start | bytes 12292
  24.7 52.3 %copy-start.4 = (s32[16]{0:T(128)S(1)}, s32[16]{0:T(128)}, u32[]{:S(2)}) copy-start(s32[16]{0:T(128)} %param.8) | copy-start | bytes 196
  24.7 64.5 %copy-start = (bf16[512,1024]{1,0:T(8,128)(2,1)S(1)}, bf16[512,1024]{1,0:T(8,128)(2,1)}, u32[]{:S(2)}) copy-start(bf16[512,1024]{1,0:T(8,128)(2,1)} %constant.13.clone.lag_ref) | copy-start | bytes 3145732
  24.7 14.7 %collective-permute-start.2 = (bf16[128,512]{1,0:T(8,128)(2,1)S(1)}, bf16[128,512]{1,0:T(8,128)(2,1)S(1)}, u32[]{:S(2)}, u32[]{:S(2)}) collective-permute-start(bf16[128,512]{1,0:T(8,128)(2,1)S(1)} %gather_days.1.refs_4_), channel_id=1, source_target_pairs={{0,64},{64,128},{128,192},{192,256},{256,320},{320,384},{384,448},... | collective-permute-start | bytes 393224 | tf_op jit(solution)/shard_map/ppermute | solution.py:288
  29.0 17.8 %collective-permute-start = (bf16[128,512]{1,0:T(8,128)(2,1)S(1)}, bf16[128,512]{1,0:T(8,128)(2,1)S(1)}, u32[]{:S(2)}, u32[]{:S(2)}) collective-permute-start(bf16[128,512]{1,0:T(8,128)(2,1)S(1)} %gather_days.1.refs_4_), channel_id=1, source_target_pairs={{0,384},{64,448},{128,0},{192,64},{256,128},{320,192},{384,256},{4... | collective-permute-start | bytes 393224 | tf_op jit(solution)/shard_map/ppermute | solution.py:288
  39.4 14.5 %collective-permute-start.3 = (bf16[128,512]{1,0:T(8,128)(2,1)S(1)}, bf16[128,512]{1,0:T(8,128)(2,1)S(1)}, u32[]{:S(2)}, u32[]{:S(2)}) collective-permute-start(bf16[128,512]{1,0:T(8,128)(2,1)S(1)} %collective-permute-done.2.refs_3_), channel_id=1, source_target_pairs={{0,64},{64,128},{128,192},{192,256},{256,320},{320,384},{384,448},... | collective-permute-start | bytes 393224 | tf_op jit(solution)/shard_map/ppermute | solution.py:288
  46.8 13.6 %collective-permute-start.1 = (bf16[128,512]{1,0:T(8,128)(2,1)S(1)}, bf16[128,512]{1,0:T(8,128)(2,1)S(1)}, u32[]{:S(2)}, u32[]{:S(2)}) collective-permute-start(bf16[128,512]{1,0:T(8,128)(2,1)S(1)} %collective-permute-done), channel_id=1, source_target_pairs={{0,384},{64,448},{128,0},{192,64},{256,128},{320,192},{384,256},{4... | collective-permute-start | bytes 393224 | tf_op jit(solution)/shard_map/ppermute | solution.py:288
  53.9 12.1 %collective-permute-start.4 = (bf16[128,512]{1,0:T(8,128)(2,1)S(1)}, bf16[128,512]{1,0:T(8,128)(2,1)S(1)}, u32[]{:S(2)}, u32[]{:S(2)}) collective-permute-start(bf16[128,512]{1,0:T(8,128)(2,1)S(1)} %collective-permute-done.3.refs_2_), channel_id=1, source_target_pairs={{0,64},{64,128},{128,192},{192,256},{256,320},{320,384},{384,448},... | collective-permute-start | bytes 393224 | tf_op jit(solution)/shard_map/ppermute | solution.py:288
  69.5 19.7 %all-to-all-start.1 = ((bf16[64,32,128]{2,1,0:T(8,128)(2,1)}), bf16[64,32,128]{2,1,0:T(8,128)(2,1)S(1)}, u32[]{:S(2)}, u32[]{:S(2)}) async-start(bf16[64,32,128]{2,1,0:T(8,128)(2,1)} %cross.1), calls=%async_computation.1 | async-start | bytes 1048576 | tf_op jit(solution)/shard_map/all_to_all | solution.py:315

commit v7 on v6

--- a/solution.py
+++ b/solution.py
@@ -287,12 +287,10 @@
         pairs = [(source, (source + steps) % GROUPS) for source in range(GROUPS)]
         return lax.ppermute(piece, "zq", pairs)
 
-    half_way = moved(own, -(GROUPS - BACK) // 2)
-    met = [own, moved(own, 1)]
-    far = moved(half_way, -(GROUPS - BACK) // 2)
-    for _ in range(BACK - 2):
+    met = [own]
+    for _ in range(BACK - 1):
         met.append(moved(met[-1], 1))
-    met.append(far)
+    met.append(moved(own, BACK))
 
     choice = (
         lax.broadcasted_iota(jnp.int32, (PAIRS, PAIRS), 0) == pair_order[None, :]

time: 91.7 us -> 94.2 us (1.027)
  waiting for transfers between devices: 23.8 us -> 33.7 us
  starting transfers between devices: 36.2 us -> 28.8 us
    ppermute x5 -> x4, waiting for transfers between devices: 11.7 us -> 21.6 us  [moved(): return lax.ppermute(piece, 'zq', pairs)]
    ppermute x5 -> x4, starting transfers between devices: 28.7 us -> 22 us  [moved(): return lax.ppermute(piece, 'zq', pairs)]
  transfers between devices with their start and end apart: 6 -> 5, of which waited for: 4 -> 3; matrix products, arithmetic and copies ran while one was open for 1% -> 1% of each run, Pallas kernels for 0% -> 0%
where the time goes in v7:
time: 94.2 us; the launch traced here: 93.8 us
  waiting for transfers between devices  33.7 us (36%)
  starting transfers between devices  28.8 us (31%)
  blocking collectives  19.6 us (21%)
  Pallas kernels  10.6 us (11%)
  other arithmetic  1 us (1%)
    ppermute x4, starting transfers between devices, moved(): return lax.ppermute(piece, 'zq', pairs)  22 us
    ppermute x4, waiting for transfers between devices, moved(): return lax.ppermute(piece, 'zq', pairs)  21.6 us
    all_to_all x1, blocking collectives, shards(): lax.all_to_all(spectra, group_axes, 0, 0, tiled=True)  19.6 us
    all_to_all x1, waiting for transfers between devices, shards(): by_pair = lax.all_to_all(chosen, group_axes, 0, 0, tiled=True)  12.1 us
    all_to_all x1, starting transfers between devices, shards(): by_pair = lax.all_to_all(chosen, group_axes, 0, 0, tiled=True)  6.81 us
    pallas_call x1, Pallas kernels, shards(): pl.pallas_call(spectra_kernel, in_specs=[pl.BlockSpec(memory_space=pltpu....  4.82 us
    pallas_call x1, Pallas kernels, shards(): pl.pallas_call(cross_kernel, in_specs=vmem_specs(BACK + 4), out_specs=pl....  3.39 us
    pallas_call x1, Pallas kernels, shards(): pl.pallas_call(lag_kernel, in_specs=[pl.BlockSpec(memory_space=pltpu.SMEM...  2.16 us
  transfers between devices with their start and end apart: 5, of which 3 were waited for; matrix products, arithmetic and copies ran while one was open for 1% of the time, Pallas kernels for 0%

profile of v7, /device:TPU:1, one launch (start us, length us, event | category | flops | bytes accessed | tf_op | source)
XLA Modules:
  0.0 93.8 jit_solution(7126199449666408421)
XLA Ops:
  0.0 0.0 copy-start.1
  0.0 0.0 copy-start.2
  0.0 0.0 copy-start.3
  0.0 4.8 %spectra.1 = bf16[64,4,256]{2,1,0:T(4,128)(2,1)} custom-call(bf16[32,8,6000]{2,1,0:T(8,128)(2,1)} %records_ref.1, f32[568,256]{1,0:T(8,128)} %constant.10.clone.parts_ref), custom_call_target="tpu_custom_call" | custom-call | tf_op jit(solution)/shard_map/spectra/pallas_call | solution.py:260
  4.8 19.6 %all_to_all.10 = bf16[64,4,256]{2,1,0:T(4,128)(2,1)S(1)} all-to-all(bf16[64,4,256]{2,1,0:T(4,128)(2,1)} %spectra.1), channel_id=1, replica_groups=mesh['zq'=8,'zr'=2,'xh'=2,'day'=16] {'zr','xh','day'}, dimensions={0} | all-to-all | bytes 262144 | tf_op jit(solution)/shard_map/all_to_all | solution.py:274
  24.5 0.2 gather_days.1.refs_4_
  24.7 0.0 copy-start.4
  24.7 0.0 copy-start
  24.7 4.3 %collective-permute-start.1 = (bf16[128,512]{1,0:T(8,128)(2,1)S(1)}, bf16[128,512]{1,0:T(8,128)(2,1)S(1)}, u32[]{:S(2)}, u32[]{:S(2)}) collective-permute-start(bf16[128,512]{1,0:T(8,128)(2,1)S(1)} %gather_days.1.refs_4_), channel_id=1, source_target_pairs={{0,64},{64,128},{128,192},{192,256},{256,320},{320,384},{384,448},... | collective-permute-start | bytes 393224 | tf_op jit(solution)/shard_map/ppermute | solution.py:288
  29.0 10.4 %collective-permute-done.1.refs_3_ = bf16[128,512]{1,0:T(8,128)(2,1)S(1)} collective-permute-done((bf16[128,512]{1,0:T(8,128)(2,1)S(1)}, bf16[128,512]{1,0:T(8,128)(2,1)S(1)}, u32[]{:S(2)}, u32[]{:S(2)}) %collective-permute-start.1) | collective-permute-done | bytes 131104 | tf_op jit(solution)/shard_map/ppermute | solution.py:288
  39.4 1.9 %collective-permute-start.2 = (bf16[128,512]{1,0:T(8,128)(2,1)S(1)}, bf16[128,512]{1,0:T(8,128)(2,1)S(1)}, u32[]{:S(2)}, u32[]{:S(2)}) collective-permute-start(bf16[128,512]{1,0:T(8,128)(2,1)S(1)} %collective-permute-done.1.refs_3_), channel_id=1, source_target_pairs={{0,64},{64,128},{128,192},{192,256},{256,320},{320,384},{384,448},... | collective-permute-start | bytes 393224 | tf_op jit(solution)/shard_map/ppermute | solution.py:288
  41.3 10.4 %collective-permute-start = (bf16[128,512]{1,0:T(8,128)(2,1)S(1)}, bf16[128,512]{1,0:T(8,128)(2,1)S(1)}, u32[]{:S(2)}, u32[]{:S(2)}) collective-permute-start(bf16[128,512]{1,0:T(8,128)(2,1)S(1)} %gather_days.1.refs_4_), channel_id=1, source_target_pairs={{0,256},{64,320},{128,384},{192,448},{256,0},{320,64},{384,128},{4... | collective-permute-start | bytes 393224 | tf_op jit(solution)/shard_map/ppermute | solution.py:288
  51.7 0.0 collective-permute-done.2.refs_2_
  51.7 5.4 %collective-permute-start.3 = (bf16[128,512]{1,0:T(8,128)(2,1)S(1)}, bf16[128,512]{1,0:T(8,128)(2,1)S(1)}, u32[]{:S(2)}, u32[]{:S(2)}) collective-permute-start(bf16[128,512]{1,0:T(8,128)(2,1)S(1)} %collective-permute-done.2.refs_2_), channel_id=1, source_target_pairs={{0,64},{64,128},{128,192},{192,256},{256,320},{320,384},{384,448},... | collective-permute-start | bytes 393224 | tf_op jit(solution)/shard_map/ppermute | solution.py:288
  57.1 0.0 copy-done.3
  57.1 0.9 fusion.refs_7_
  58.0 0.0 collective-permute-done.refs_0_
  58.0 11.2 %collective-permute-done.3.refs_1_ = bf16[128,512]{1,0:T(8,128)(2,1)S(1)} collective-permute-done((bf16[128,512]{1,0:T(8,128)(2,1)S(1)}, bf16[128,512]{1,0:T(8,128)(2,1)S(1)}, u32[]{:S(2)}, u32[]{:S(2)}) %collective-permute-start.3) | collective-permute-done | bytes 131104 | tf_op jit(solution)/shard_map/ppermute | solution.py:288
  69.3 0.0 copy-done.1
  69.3 0.0 copy-done.2
  69.3 3.4 %cross.1 = bf16[64,32,128]{2,1,0:T(8,128)(2,1)} custom-call(bf16[128,512]{1,0:T(8,128)(2,1)S(1)} %collective-permute-done.refs_0_, bf16[128,512]{1,0:T(8,128)(2,1)S(1)} %collective-permute-done.3.refs_1_, bf16[128,512]{1,0:T(8,128)(2,1)S(1)} %collective-permute-done.2.refs_2_, bf16[128,512]{1,0:T(8,128)(2,1)S(1)} %collective-permute-done.1.refs_3_, ...), custom_call_target="tpu_custom_call" | custom-call | tf_op jit(solution)/shard_map/cross/pallas_call | solution.py:299
  72.7 6.8 %all-to-all-start.1 = ((bf16[64,32,128]{2,1,0:T(8,128)(2,1)}), bf16[64,32,128]{2,1,0:T(8,128)(2,1)S(1)}, u32[]{:S(2)}, u32[]{:S(2)}) async-start(bf16[64,32,128]{2,1,0:T(8,128)(2,1)} %cross.1), calls=%async_computation.1 | async-start | bytes 1048576 | tf_op jit(solution)/shard_map/all_to_all | solution.py:313
  79.5 0.0 copy-done.4
  79.5 0.1 select_reduce_fusion.slot_ref
  79.6 12.1 %all-to-all-done.1.r_ref = bf16[64,32,128]{2,1,0:T(8,128)(2,1)S(1)} async-done(((bf16[64,32,128]{2,1,0:T(8,128)(2,1)}), bf16[64,32,128]{2,1,0:T(8,128)(2,1)S(1)}, u32[]{:S(2)}, u32[]{:S(2)}) %all-to-all-start.1) | async-done | bytes 524320 | tf_op jit(solution)/shard_map/all_to_all | solution.py:313
  91.7 0.0 copy-done
  91.7 2.2 %lags.1 = f32[16,64,101]{2,1,0:T(8,128)} custom-call(s32[16]{0:T(128)S(1)} %select_reduce_fusion.slot_ref, bf16[64,32,128]{2,1,0:T(8,128)(2,1)S(1)} %all-to-all-done.1.r_ref, bf16[512,1024]{1,0:T(8,128)(2,1)S(1)} %copy-done), custom_call_target="tpu_custom_call" | custom-call | tf_op jit(solution)/shard_map/lags/pallas_call | solution.py:320
  (1 shorter events, 0.0 us)
Async XLA Ops:
  0.0 69.3 %copy-start.1 = (bf16[256,320]{1,0:T(8,128)(2,1)S(1)}, bf16[256,320]{1,0:T(8,128)(2,1)}, u32[]{:S(2)}) copy-start(bf16[256,320]{1,0:T(8,128)(2,1)} %constant.12.clone.refs_6_) | copy-start | bytes 491524
  0.0 69.3 %copy-start.2 = (bf16[512,128]{1,0:T(8,128)(2,1)S(1)}, bf16[512,128]{1,0:T(8,128)(2,1)}, u32[]{:S(2)}) copy-start(bf16[512,128]{1,0:T(8,128)(2,1)} %constant.11.clone.refs_5_) | copy-start | bytes 393220
  0.0 57.1 %copy-start.3 = (s32[1024]{0:T(1024)S(1)}, s32[1024]{0:T(1024)}, u32[]{:S(2)}) copy-start(s32[1024]{0:T(1024)} %param.9) | copy-start | bytes 12292
  24.7 54.8 %copy-start.4 = (s32[16]{0:T(128)S(1)}, s32[16]{0:T(128)}, u32[]{:S(2)}) copy-start(s32[16]{0:T(128)} %param.8) | copy-start | bytes 196
  24.7 67.0 %copy-start = (bf16[512,1024]{1,0:T(8,128)(2,1)S(1)}, bf16[512,1024]{1,0:T(8,128)(2,1)}, u32[]{:S(2)}) copy-start(bf16[512,1024]{1,0:T(8,128)(2,1)} %constant.13.clone.lag_ref) | copy-start | bytes 3145732
  24.7 14.7 %collective-permute-start.1 = (bf16[128,512]{1,0:T(8,128)(2,1)S(1)}, bf16[128,512]{1,0:T(8,128)(2,1)S(1)}, u32[]{:S(2)}, u32[]{:S(2)}) collective-permute-start(bf16[128,512]{1,0:T(8,128)(2,1)S(1)} %gather_days.1.refs_4_), channel_id=1, source_target_pairs={{0,64},{64,128},{128,192},{192,256},{256,320},{320,384},{384,448},... | collective-permute-start | bytes 393224 | tf_op jit(solution)/shard_map/ppermute | solution.py:288
  39.4 12.3 %collective-permute-start.2 = (bf16[128,512]{1,0:T(8,128)(2,1)S(1)}, bf16[128,512]{1,0:T(8,128)(2,1)S(1)}, u32[]{:S(2)}, u32[]{:S(2)}) collective-permute-start(bf16[128,512]{1,0:T(8,128)(2,1)S(1)} %collective-permute-done.1.refs_3_), channel_id=1, source_target_pairs={{0,64},{64,128},{128,192},{192,256},{256,320},{320,384},{384,448},... | collective-permute-start | bytes 393224 | tf_op jit(solution)/shard_map/ppermute | solution.py:288
  41.3 16.7 %collective-permute-start = (bf16[128,512]{1,0:T(8,128)(2,1)S(1)}, bf16[128,512]{1,0:T(8,128)(2,1)S(1)}, u32[]{:S(2)}, u32[]{:S(2)}) collective-permute-start(bf16[128,512]{1,0:T(8,128)(2,1)S(1)} %gather_days.1.refs_4_), channel_id=1, source_target_pairs={{0,256},{64,320},{128,384},{192,448},{256,0},{320,64},{384,128},{4... | collective-permute-start | bytes 393224 | tf_op jit(solution)/shard_map/ppermute | solution.py:288
  51.7 17.6 %collective-permute-start.3 = (bf16[128,512]{1,0:T(8,128)(2,1)S(1)}, bf16[128,512]{1,0:T(8,128)(2,1)S(1)}, u32[]{:S(2)}, u32[]{:S(2)}) collective-permute-start(bf16[128,512]{1,0:T(8,128)(2,1)S(1)} %collective-permute-done.2.refs_2_), channel_id=1, source_target_pairs={{0,64},{64,128},{128,192},{192,256},{256,320},{320,384},{384,448},... | collective-permute-start | bytes 393224 | tf_op jit(solution)/shard_map/ppermute | solution.py:288
  72.7 19.0 %all-to-all-start.1 = ((bf16[64,32,128]{2,1,0:T(8,128)(2,1)}), bf16[64,32,128]{2,1,0:T(8,128)(2,1)S(1)}, u32[]{:S(2)}, u32[]{:S(2)}) async-start(bf16[64,32,128]{2,1,0:T(8,128)(2,1)} %cross.1), calls=%async_computation.1 | async-start | bytes 1048576 | tf_op jit(solution)/shard_map/all_to_all | solution.py:313
